TPU v7x, 256 devices: a whole 4x4x8 slice. The times are simulated.
256 devices in a mesh: row: 64 (over x, z, core), col: 4 (over y).
Axes of the slice: x: 4, y: 4, z: 8, core: 2. Of those that a mesh axis runs over, the one named last changes fastest.
Arguments:
- h_blocks: bfloat16 [3072, 128, 128], P(('row', 'col')), may hold values from -0.125 to 0.125
- block_ids: int32 [256, 64], replicated, may hold values from 0 to 3071, as said below
- pattern: int32 [256, 8, 8], P(('row', 'col')), may hold values 0 or 1
- result_grad: bfloat16 [262144, 128], P(('row', 'col')), may hold values from -6 to 6
Outputs:
- grad_blocks: float32 [3072, 128, 128], P(('row', 'col'))
Inputs may be any that keep to these rules, and one draw needn't show every extreme that they name: `block_ids`: submatrix s sits on device s (devices numbered over row, then col). Stored block i lies on device i // 12 in its local slot i % 12. Of the 64 blocks of one submatrix, exactly 16 lie on devices of each col index and at most 1 on any one device. Of all blocks that the submatrices of one row index take from devices of one col index, at most 1 lie on devices of any one row index. Both bounds are reached in every draw.
All inputs are finite; a program needn't handle non-finite values. No bound on the sum of `pattern` on one device may be relied on, other than what follows from the above.
Results may differ from a plain program's by a relative error of at most 0.0034.
Values may be sent and summed in bfloat16 or wider, within the bound.
No kernel may reach another device: no remote copies, remote signals or barrier semaphores. Data moves between devices by JAX's collectives and lax.ppermute only.
A program may use at most 128 MiB of HBM per device.

v0:
```python
import jax
import jax.numpy as jnp
from jax import lax
from jax.sharding import PartitionSpec as P


def multiply(former, latter):
    return jnp.dot(former, latter, preferred_element_type=jnp.float32)


def left_transposed(former, latter):
    return lax.dot_general(
        former, latter, (((0,), (0,)), ((), ())), preferred_element_type=jnp.float32
    )


def right_transposed(former, latter):
    return lax.dot_general(
        former, latter, (((1,), (1,)), ((), ())), preferred_element_type=jnp.float32
    )


def assemble(blocks, block_edge, block_width):
    full_order = block_edge * block_width
    return (
        blocks.reshape(block_edge, block_edge, block_width, block_width)
        .transpose(0, 2, 1, 3)
        .reshape(full_order, full_order)
    )


def split_blocks(matrix, block_edge, block_width):
    return (
        matrix.reshape(block_edge, block_width, block_edge, block_width)
        .transpose(0, 2, 1, 3)
        .reshape(block_edge * block_edge, block_width, block_width)
    )


def adjoint(initial, result_cot):
    block_width = result_cot.shape[1]
    square = multiply(initial, initial).astype(jnp.bfloat16)
    iterate = (1.5 * initial.astype(jnp.float32) - 0.5 * multiply(initial, square)).astype(
        jnp.bfloat16
    )
    lead_cols = iterate[:, :block_width]
    pulled = left_transposed(iterate, result_cot).astype(jnp.bfloat16)
    lead_square = multiply(iterate, lead_cols).astype(jnp.bfloat16)
    crossed = right_transposed(
        jnp.concatenate([pulled, result_cot], axis=1),
        jnp.concatenate([lead_cols, lead_square], axis=1),
    )
    nearby = left_transposed(iterate, pulled)
    head_part = 1.5 * result_cot.astype(jnp.float32) - 0.5 * nearby - 0.5 * crossed[:, :block_width]
    cot_iterate = jnp.concatenate([head_part, -0.5 * crossed[:, block_width:]], axis=1).astype(
        jnp.bfloat16
    )
    inner_part = left_transposed(initial, cot_iterate).astype(jnp.bfloat16)
    term_left = left_transposed(square, cot_iterate)
    term_middle = right_transposed(inner_part, initial)
    term_right = right_transposed(cot_iterate, square)
    return 1.5 * cot_iterate.astype(jnp.float32) - 0.5 * (term_left + term_middle + term_right)


def earlier_same(labels):
    span_size = labels.shape[-1]
    counter = jnp.arange(span_size)
    before = counter[None, :] < counter[:, None]
    matches = labels[..., :, None] == labels[..., None, :]
    return jnp.sum(jnp.logical_and(matches, before).astype(jnp.int32), axis=-1)


def shards(h_blocks, block_ids, pattern, result_grad):
    row_count = lax.axis_size("row")
    col_count = lax.axis_size("col")
    my_row = lax.axis_index("row")
    my_col = lax.axis_index("col")
    myself = my_row * col_count + my_col
    slot_count = h_blocks.shape[0]
    block_width = h_blocks.shape[1]
    block_edge = pattern.shape[1]
    sub_count, entries = block_ids.shape
    col_room = entries // col_count
    pair_room = (col_room + row_count - 1) // row_count
    owner = block_ids // slot_count
    local_slot = block_ids % slot_count
    sub_index = jnp.broadcast_to(jnp.arange(sub_count, dtype=jnp.int32)[:, None], block_ids.shape)
    keep_flags = pattern.reshape(entries, 1, 1)
    entry_index = jnp.arange(entries, dtype=jnp.int32)
    pair_rank = earlier_same(owner)
    pair_target = jnp.where(
        owner == myself, sub_index * pair_room + pair_rank, sub_count * pair_room
    )
    slot_table = (
        jnp.full((sub_count * pair_room,), slot_count, jnp.int32)
        .at[pair_target.reshape(-1)]
        .set(local_slot.reshape(-1), mode="drop")
    )
    outgoing = jnp.take(h_blocks, slot_table, axis=0, mode="fill", fill_value=0)
    outgoing = outgoing.reshape(row_count, col_count, pair_room, block_width, block_width)
    arrived = lax.all_to_all(
        lax.all_to_all(outgoing, "row", split_axis=0, concat_axis=0, tiled=True),
        "col",
        split_axis=1,
        concat_axis=1,
        tiled=True,
    )
    arrived = arrived.reshape(sub_count * pair_room, block_width, block_width)
    my_owner = lax.dynamic_index_in_dim(owner, myself, 0, keepdims=False)
    my_pair = lax.dynamic_index_in_dim(pair_rank, myself, 0, keepdims=False)
    fetched = jnp.take(arrived, my_owner * pair_room + my_pair, axis=0)
    initial = assemble(fetched * keep_flags.astype(jnp.bfloat16), block_edge, block_width)
    cot_initial = adjoint(initial, result_grad)
    pieces = split_blocks(cot_initial, block_edge, block_width) * keep_flags.astype(jnp.float32)
    source_pick = (
        jnp.full((sub_count * pair_room,), entries, jnp.int32)
        .at[my_owner * pair_room + my_pair]
        .set(entry_index)
    )
    leaving = jnp.take(pieces, source_pick, axis=0, mode="fill", fill_value=0)
    leaving = leaving.reshape(row_count, col_count, pair_room, block_width, block_width)
    landed = lax.all_to_all(
        lax.all_to_all(leaving, "row", split_axis=0, concat_axis=0, tiled=True),
        "col",
        split_axis=1,
        concat_axis=1,
        tiled=True,
    )
    landed = landed.reshape(sub_count * pair_room, block_width, block_width)
    weights = jax.nn.one_hot(slot_table, slot_count, dtype=jnp.float32)
    return jnp.einsum("rs,rab->sab", weights, landed, precision=lax.Precision.HIGHEST)


def solution(mesh):
    in_specs = (
        P(("row", "col"), None, None),
        P(),
        P(("row", "col"), None, None),
        P(("row", "col"), None),
    )
    out_specs = P(("row", "col"), None, None)
    return jax.shard_map(shards, mesh=mesh, in_specs=in_specs, out_specs=out_specs, check_vma=False)
```

profile of v0, /device:TPU:1, one launch (start us, length us, event | category | flops | bytes accessed | tf_op | source)
XLA Modules:
  0.0 1069.1 jit_solution(5546985266021366787)
XLA Ops:
  3.3 60.3 %scatter_custom_fusion = s32[256]{0:T(256)S(1)} fusion(s32[16384]{0:T(1024)S(1)} %bitcast.66, s32[16384]{0:T(1024)S(1)} %reshape.195, s32[]{:T(128)} %constant.48.clone.1), kind=kCustom, calls=%fused_computation.70 | custom fusion | bytes 1028 | tf_op jit(solution)/shard_map/scatter | solution.py:97
  63.8 8.4 gather_fusion
  72.2 7.3 broadcast_select_fusion
  79.4 199.2 %all_to_all.20 = bf16[64,4,1,128,128]{4,3,1,2,0:T(8,128)(2,1)} all-to-all(bf16[64,4,1,128,128]{4,3,1,2,0:T(8,128)(2,1)} %broadcast_select_fusion), channel_id=1, replica_groups=mesh['row'=64,'col'=4] {'row'}, dimensions={0} | all-to-all | bytes 16777216 | tf_op jit(solution)/shard_map/all_to_all | solution.py:102
  278.6 10.3 copy.64
  288.9 5.8 all-to-all-start.1
  296.4 91.8 %all-to-all-done.1 = bf16[64,4,1,128,128]{4,3,0,2,1:T(8,128)(2,1)} async-done(((bf16[64,4,1,128,128]{4,3,0,2,1:T(8,128)(2,1)}), bf16[64,4,1,128,128]{4,3,0,2,1:T(8,128)(2,1)}, u32[]{:S(2)}, u32[]{:S(2)}) %all-to-all-start.1) | async-done | bytes 8388640 | tf_op jit(solution)/shard_map/all_to_all | solution.py:101
  388.2 10.3 copy.65
  398.6 4.3 gather_fusion.1
  404.5 3.2 copy.66
  410.1 2.7 subtract_convert_fusion
  417.5 8.0 fusion.3
  425.5 5.0 fusion.23
  430.6 2.7 subtract_bitcast_fusion
  433.3 3.0 copy.80
  436.3 5.4 copy.71
  441.7 4.5 bitcast_multiply_fusion
  446.1 13.7 %gather_fusion.2 = f32[256,128,128]{2,1,0:T(8,128)} fusion(f32[64,128,128]{2,1,0:T(8,128)} %bitcast_multiply_fusion, s32[1024]{0:T(1024)S(1)} %pad_clamp_fusion), kind=kCustom, calls=%fused_computation.2 | custom fusion | bytes 33555456 | tf_op jit(solution)/shard_map/jit(_take)/gather | solution.py:120
  459.8 19.1 %copy_select_fusion = f32[64,4,1,128,128]{4,1,3,2,0:T(4,128)S(1)} fusion(f32[64,4,1,128,128]{4,3,1,0,2:T(8,128)} %bitcast.57, pred[64,4]{1,0:T(8,128)(4,1)S(1)} %broadcast_in_dim.67), kind=kLoop, calls=%fused_computation.5 | loop fusion | flops 4194304 | bytes 33554688 | tf_op jit(solution)/shard_map/jit(_take)/select_n | solution.py:120
  479.0 372.3 %all_to_all.21 = f32[64,4,1,128,128]{4,1,3,2,0:T(4,128)S(1)} all-to-all(f32[64,4,1,128,128]{4,1,3,2,0:T(4,128)S(1)} %copy_select_fusion), channel_id=1, replica_groups=mesh['row'=64,'col'=4] {'row'}, dimensions={0} | all-to-all | bytes 33554432 | tf_op jit(solution)/shard_map/all_to_all | solution.py:123
  851.3 11.7 %copy.73 = f32[64,4,1,128,128]{4,0,3,2,1:T(8,128)} copy(f32[64,4,1,128,128]{4,1,3,2,0:T(4,128)S(1)} %all_to_all.21) | data formatting | bytes 33554432 | tf_op jit(solution)/shard_map/all_to_all | solution.py:123
  863.0 188.1 %all_to_all.22 = f32[64,4,1,128,128]{4,0,3,2,1:T(8,128)S(1)} all-to-all(f32[64,4,1,128,128]{4,0,3,2,1:T(8,128)} %copy.73), channel_id=1, replica_groups=mesh['row'=64,'col'=4] {'col'}, dimensions={1} | all-to-all | bytes 33554432 | tf_op jit(solution)/shard_map/all_to_all | solution.py:122
  1051.1 11.0 %copy.74 = f32[64,4,1,128,128]{4,1,0,3,2:T(4,128)S(1)} copy(f32[64,4,1,128,128]{4,0,3,2,1:T(8,128)S(1)} %all_to_all.22) | data formatting | bytes 33554432 | tf_op jit(solution)/shard_map/all_to_all | solution.py:122
  1062.1 5.7 fusion.33
  (52 shorter events, 14.8 us)
Async XLA Ops:
  0.0 63.8 %copy-start = (bf16[12,128,128]{2,1,0:T(8,128)(2,1)S(1)}, bf16[12,128,128]{2,1,0:T(8,128)(2,1)}, u32[]{:S(2)}) copy-start(bf16[12,128,128]{2,1,0:T(8,128)(2,1)} %param.4) | copy-start | bytes 1179652
  288.9 5.8 copy-start.4
  288.9 7.3 copy-start.3
  288.9 99.3 %all-to-all-start.1 = ((bf16[64,4,1,128,128]{4,3,0,2,1:T(8,128)(2,1)}), bf16[64,4,1,128,128]{4,3,0,2,1:T(8,128)(2,1)}, u32[]{:S(2)}, u32[]{:S(2)}) async-start(bf16[64,4,1,128,128]{4,3,0,2,1:T(8,128)(2,1)} %copy.64), calls=%async_computation.1 | async-start | bytes 16777216 | tf_op jit(solution)/shard_map/all_to_all | solution.py:101
  410.1 2.7 copy-start.6
  425.5 5.0 copy-start.2
  425.5 5.0 copy-start.5
  425.5 5.0 copy-start.7
  1062.1 6.8 copy-start.1
where the time goes:
time: 1080 us; the launch traced here: 1070 us
  blocking collectives  760 us (70%)
  local copies, waits for them, and re-layouts  145 us (13%)
  waiting for transfers between devices  91.8 us (8%)
  other arithmetic  37.3 us (3%)
  matrix products  29.4 us (3%)
    all_to_all x1, blocking collectives, shards(): lax.all_to_all(leaving, 'row', split_axis=0, concat_axis=0, tiled=True)  372 us
    all_to_all x1, blocking collectives, shards(): lax.all_to_all(outgoing, 'row', split_axis=0, concat_axis=0, tiled=True)  199 us
    all_to_all x1, blocking collectives, shards(): lax.all_to_all(lax.all_to_all(leaving, 'row', split_axis=0, concat_axis=0...  188 us
    all_to_all x1, waiting for transfers between devices, shards(): lax.all_to_all(lax.all_to_all(outgoing, 'row', split_axis=0, concat_axis=...  91.8 us
    scatter x1, local copies, waits for them, and re-layouts, shards(): slot_table = jnp.full((sub_count * pair_room,), slot_count, jnp.int32).at...  60.3 us
  transfers between devices with their start and end apart: 1, of which 1 were waited for; matrix products, arithmetic and copies ran while one was open for 0% of the time, Pallas kernels for 0%

commit v1 on v0

v1 whole, which is shorter than its diff:
```python
import jax
import jax.numpy as jnp
from jax import lax
from jax.sharding import PartitionSpec as P


def multiply(former, latter):
    return jnp.dot(former, latter, preferred_element_type=jnp.float32)


def left_transposed(former, latter):
    return lax.dot_general(
        former, latter, (((0,), (0,)), ((), ())), preferred_element_type=jnp.float32
    )


def right_transposed(former, latter):
    return lax.dot_general(
        former, latter, (((1,), (1,)), ((), ())), preferred_element_type=jnp.float32
    )


def assemble(blocks, block_edge, block_width):
    full_order = block_edge * block_width
    return (
        blocks.reshape(block_edge, block_edge, block_width, block_width)
        .transpose(0, 2, 1, 3)
        .reshape(full_order, full_order)
    )


def split_blocks(matrix, block_edge, block_width):
    return (
        matrix.reshape(block_edge, block_width, block_edge, block_width)
        .transpose(0, 2, 1, 3)
        .reshape(block_edge * block_edge, block_width, block_width)
    )


def adjoint(initial, result_cot):
    block_width = result_cot.shape[1]
    square = multiply(initial, initial).astype(jnp.bfloat16)
    iterate = (1.5 * initial.astype(jnp.float32) - 0.5 * multiply(initial, square)).astype(
        jnp.bfloat16
    )
    lead_cols = iterate[:, :block_width]
    pulled = left_transposed(iterate, result_cot).astype(jnp.bfloat16)
    lead_square = multiply(iterate, lead_cols).astype(jnp.bfloat16)
    crossed = right_transposed(
        jnp.concatenate([pulled, result_cot], axis=1),
        jnp.concatenate([lead_cols, lead_square], axis=1),
    )
    nearby = left_transposed(iterate, pulled)
    head_part = 1.5 * result_cot.astype(jnp.float32) - 0.5 * nearby - 0.5 * crossed[:, :block_width]
    cot_iterate = jnp.concatenate([head_part, -0.5 * crossed[:, block_width:]], axis=1).astype(
        jnp.bfloat16
    )
    inner_part = left_transposed(initial, cot_iterate).astype(jnp.bfloat16)
    term_left = left_transposed(square, cot_iterate)
    term_middle = right_transposed(inner_part, initial)
    term_right = right_transposed(cot_iterate, square)
    return 1.5 * cot_iterate.astype(jnp.float32) - 0.5 * (term_left + term_middle + term_right)


def shards(h_blocks, block_ids, pattern, result_grad):
    row_count = lax.axis_size("row")
    col_count = lax.axis_size("col")
    my_row = lax.axis_index("row")
    my_col = lax.axis_index("col")
    slot_count, block_width, _ = h_blocks.shape
    block_edge = pattern.shape[1]
    entries = block_ids.shape[1]
    room = entries // col_count
    owner = block_ids // slot_count
    slot = block_ids % slot_count
    mine = (owner == my_row * col_count + my_col).reshape(row_count, -1)
    slot_of_row = jnp.sum(jnp.where(mine, slot.reshape(row_count, -1), 0), axis=1)
    near = lax.dynamic_slice_in_dim(owner, my_row * col_count, col_count, 0)
    near_row = near // col_count
    near_col = near % col_count
    ranks = jnp.arange(room)
    taken = near_col == my_col
    place = jnp.cumsum(taken.astype(jnp.int32), axis=1) - 1
    picks = jnp.logical_and(taken[:, :, None], place[:, :, None] == ranks)
    row_at = jnp.sum(jnp.where(picks, near_row[:, :, None], 0), axis=1).reshape(-1)
    where_row = jnp.sum(
        jnp.where(
            row_at[None, :] == jnp.arange(row_count)[:, None], jnp.arange(entries)[None, :], 0
        ),
        axis=1,
    )
    my_cols = lax.dynamic_index_in_dim(near_col, my_col, 0, keepdims=False)
    on_col = my_cols[None, :] == jnp.arange(col_count)[:, None]
    rank = jnp.sum(jnp.where(on_col, jnp.cumsum(on_col.astype(jnp.int32), axis=1) - 1, 0), axis=0)
    spot = my_cols * room + rank
    entry_at = jnp.sum(
        jnp.where(spot[None, :] == jnp.arange(entries)[:, None], jnp.arange(entries)[None, :], 0),
        axis=1,
    )
    keep_flags = pattern.reshape(entries, 1, 1)

    def over(blocks, axis):
        return lax.all_to_all(blocks, axis, split_axis=0, concat_axis=0, tiled=True)

    arrived = over(jnp.take(h_blocks, slot_of_row, axis=0), "row")
    arrived = over(jnp.take(arrived, row_at, axis=0), "col")
    fetched = jnp.take(arrived, spot, axis=0)
    initial = assemble(fetched * keep_flags.astype(jnp.bfloat16), block_edge, block_width)
    cot_initial = adjoint(initial, result_grad)
    pieces = split_blocks(cot_initial, block_edge, block_width) * keep_flags.astype(jnp.float32)
    leaving = jnp.take(pieces.astype(jnp.bfloat16), entry_at, axis=0)
    leaving = jnp.take(over(leaving, "col"), where_row, axis=0)
    landed = over(leaving, "row")
    weights = (slot_of_row[None, :] == jnp.arange(slot_count)[:, None]).astype(jnp.bfloat16)
    return jnp.einsum("sr,rab->sab", weights, landed, preferred_element_type=jnp.float32)


def solution(mesh):
    in_specs = (
        P(("row", "col"), None, None),
        P(),
        P(("row", "col"), None, None),
        P(("row", "col"), None),
    )
    out_specs = P(("row", "col"), None, None)
    return jax.shard_map(shards, mesh=mesh, in_specs=in_specs, out_specs=out_specs, check_vma=False)
```

time: 1080 us -> 249 us (0.23)
  blocking collectives: 760 us -> 59.5 us
  local copies, waits for them, and re-layouts: 145 us -> 24.3 us
  other arithmetic: 37.3 us -> 17.1 us
  starting transfers between devices: 5.77 us -> 21.2 us
    all_to_all x3 -> x1, blocking collectives: 760 us -> 59.5 us  [over(): return lax.all_to_all(blocks, axis, split_axis=0, concat_axis=0, tiled=True)]
    scatter x2 -> x0, local copies, waits for them, and re-layouts: 61.2 us -> none  [the longest x1 60.3 us: shards(): slot_table = jnp.full((sub_count * pair_room,), slot_count, jnp.int32).at...]
    all_to_all x4 -> x0, local copies, waits for them, and re-layouts: 43.4 us -> none  [the longest x1 11.7 us: shards(): lax.all_to_all(leaving, 'row', split_axis=0, concat_axis=0, tiled=True)]
    select_n x7 -> x9, other arithmetic: 27.4 us -> 9.82 us  [the longest x2 3.2 us: shards(): leaving = jnp.take(pieces.astype(jnp.bfloat16), entry_at, axis=0)]
    gather x3 -> x5, local copies, waits for them, and re-layouts: 26.4 us -> 9.93 us  [the longest x1 2.54 us: shards(): fetched = jnp.take(arrived, spot, axis=0)]
    all_to_all x1 -> x3, starting transfers between devices: 5.77 us -> 21.2 us  [over(): return lax.all_to_all(blocks, axis, split_axis=0, concat_axis=0, tiled=True)]
    all_to_all x1 -> x3, waiting for transfers between devices: 91.8 us -> 101 us  [over(): return lax.all_to_all(blocks, axis, split_axis=0, concat_axis=0, tiled=True)]
  transfers between devices with their start and end apart: 1 -> 3, of which waited for: 1 -> 3; matrix products, arithmetic and copies ran while one was open for 0% -> 0% of each run, Pallas kernels for 0% -> 0%
where the time goes in v1:
time: 249 us; the launch traced here: 248 us
  waiting for transfers between devices  101 us (41%)
  blocking collectives  59.5 us (24%)
  matrix products  24.7 us (10%)
  local copies, waits for them, and re-layouts  24.3 us (10%)
  starting transfers between devices  21.2 us (9%)
  other arithmetic  17.1 us (7%)
    all_to_all x3, waiting for transfers between devices, over(): return lax.all_to_all(blocks, axis, split_axis=0, concat_axis=0, tiled=True)  101 us
    all_to_all x1, blocking collectives, over(): return lax.all_to_all(blocks, axis, split_axis=0, concat_axis=0, tiled=True)  59.5 us
    all_to_all x3, starting transfers between devices, over(): return lax.all_to_all(blocks, axis, split_axis=0, concat_axis=0, tiled=True)  21.2 us
    dot_general x3, matrix products, right_transposed(): lax.dot_general(former, latter, (((1,), (1,)), ((), ())), preferred_eleme...  11.4 us
    dot_general x3, matrix products, left_transposed(): lax.dot_general(former, latter, (((0,), (0,)), ((), ())), preferred_eleme...  6.52 us
    dot_general x3, matrix products, multiply(): return jnp.dot(former, latter, preferred_element_type=jnp.float32)  5.48 us
    reshape x1, local copies, waits for them, and re-layouts, split_blocks(): matrix.reshape(block_edge, block_width, block_edge, block_width)  5.4 us
  transfers between devices with their start and end apart: 3, of which 3 were waited for; matrix products, arithmetic and copies ran while one was open for 0% of the time, Pallas kernels for 0%

profile of v1, /device:TPU:1, one launch (start us, length us, event | category | flops | bytes accessed | tf_op | source)
XLA Modules:
  0.0 248.3 jit_solution(4084408780861268966)
XLA Ops:
  4.5 13.0 %all-to-all-start = ((bf16[64,128,128]{2,1,0:T(8,128)(2,1)}), bf16[64,128,128]{2,1,0:T(8,128)(2,1)S(1)}, u32[]{:S(2)}, u32[]{:S(2)}) async-start(bf16[64,128,128]{2,1,0:T(8,128)(2,1)} %broadcast_select_fusion.3), calls=%async_computation | async-start | bytes 4194304 | tf_op jit(solution)/shard_map/all_to_all | solution.py:103
  18.0 50.7 %all-to-all-done = bf16[64,128,128]{2,1,0:T(8,128)(2,1)S(1)} async-done(((bf16[64,128,128]{2,1,0:T(8,128)(2,1)}), bf16[64,128,128]{2,1,0:T(8,128)(2,1)S(1)}, u32[]{:S(2)}, u32[]{:S(2)}) %all-to-all-start) | async-done | bytes 2097184 | tf_op jit(solution)/shard_map/all_to_all | solution.py:103
  68.7 2.1 gather_fusion.1
  70.8 3.1 %broadcast_select_fusion.2 = bf16[64,128,128]{2,1,0:T(8,128)(2,1)} fusion(bf16[64,128,128]{2,1,0:T(8,128)(2,1)} %gather_fusion.1, pred[64]{0:T(512)(128)(4,1)S(1)} %compare_and_fusion.3), kind=kLoop, calls=%fused_computation.25 | loop fusion | flops 1048576 | bytes 4194368 | tf_op jit(solution)/shard_map/jit(_take)/select_n | solution.py:106
  74.0 4.6 %all-to-all-start.1 = ((bf16[64,128,128]{2,1,0:T(8,128)(2,1)}), bf16[64,128,128]{2,1,0:T(8,128)(2,1)}, u32[]{:S(2)}, u32[]{:S(2)}) async-start(bf16[64,128,128]{2,1,0:T(8,128)(2,1)} %broadcast_select_fusion.2), calls=%async_computation.1 | async-start | bytes 4194304 | tf_op jit(solution)/shard_map/all_to_all | solution.py:103
  79.0 25.6 %all-to-all-done.1 = bf16[64,128,128]{2,1,0:T(8,128)(2,1)} async-done(((bf16[64,128,128]{2,1,0:T(8,128)(2,1)}), bf16[64,128,128]{2,1,0:T(8,128)(2,1)}, u32[]{:S(2)}, u32[]{:S(2)}) %all-to-all-start.1) | async-done | bytes 2097184 | tf_op jit(solution)/shard_map/all_to_all | solution.py:103
  104.6 2.5 %gather_fusion.2 = bf16[64,128,128]{2,1,0:T(8,128)(2,1)S(1)} fusion(bf16[64,128,128]{2,1,0:T(8,128)(2,1)} %all-to-all-done.1, s32[1024]{0:T(1024)S(1)} %pad_clamp_fusion.2), kind=kCustom, calls=%fused_computation.1.clone | custom fusion | bytes 4194560 | tf_op jit(solution)/shard_map/jit(_take)/gather | solution.py:107
  108.8 3.4 %copy.43 = bf16[8,8,128,128]{2,0,3,1:T(8,128)(2,1)S(1)} copy(bf16[8,8,128,128]{3,2,1,0:T(8,128)(2,1)} %bitcast.59) | data formatting | bytes 4194304 | tf_op jit(solution)/shard_map/reshape | solution.py:26
  112.2 2.4 fusion.12
  114.6 2.6 %subtract_convert_fusion = bf16[1024,1024]{0,1:T(8,128)(2,1)S(1)} fusion(bf16[1024,1024]{1,0:T(8,128)(2,1)S(1)} %fusion.12, bf16[128,8,8,128]{3,2,1,0:T(8,128)(2,1)S(1)} %bitcast.61), kind=kOutput, calls=%fused_computation.8 | convolution fusion | flops 2152726528 | bytes 6291456 | tf_op jit(solution)/shard_map/dot_general | solution.py:8
  120.2 1.7 fusion.1
  121.9 8.0 %fusion.4 = f32[1024,1024]{0,1:T(8,128)} fusion(bf16[128,8,8,128]{3,2,1,0:T(8,128)(2,1)S(1)} %bitcast.62, bf16[1024,896]{0,1:T(8,128)(2,1)} %fusion.1, bf16[1024,128]{0,1:T(8,128)(2,1)S(1)} %fusion.25), kind=kOutput, calls=%fused_computation.13 | convolution fusion | flops 4300210176 | bytes 8388608 | tf_op jit(solution)/shard_map/dot_general | solution.py:18
  129.9 4.8 %fusion.26 = f32[1024,1024]{0,1:T(8,128)S(1)} fusion(bf16[1024,1024]{1,0:T(8,128)(2,1)} %copy-done.6, bf16[1024,896]{0,1:T(8,128)(2,1)} %fusion.1, bf16[1024,128]{0,1:T(8,128)(2,1)S(1)} %fusion.25), kind=kOutput, calls=%fused_computation.38 | convolution fusion | flops 2151677952 | bytes 8388608 | tf_op jit(solution)/shard_map/dot_general | solution.py:12
  134.8 2.7 %subtract_bitcast_fusion = f32[128,8,8,128]{3,1,2,0:T(8,128)S(1)} fusion(f32[1024,1024]{0,1:T(8,128)S(1)} %fusion.26, f32[1024,1024]{0,1:T(8,128)S(1)} %copy-done.5, bf16[1024,1024]{1,0:T(8,128)(2,1)S(1)} %copy-done.7, bf16[1024,896]{0,1:T(8,128)(2,1)S(1)} %copy-done.2, bf16[1024,128]{0,1:T(8,128)(2,1)S(1)} %fusion.25), kind=kOutput, calls=%fused_computation.7 | convolution fusion | flops 2161115136 | bytes 16777216 | tf_op jit(solution)/shard_map/dot_general | solution.py:18
  137.5 2.9 %copy.55 = f32[128,8,8,128]{3,2,1,0:T(8,128)} copy(f32[128,8,8,128]{3,1,2,0:T(8,128)S(1)} %subtract_bitcast_fusion) | data formatting | bytes 8388608
  140.4 5.4 %copy.48 = f32[8,128,8,128]{3,1,2,0:T(8,128)} copy(f32[8,128,8,128]{1,0,3,2:T(8,128)} %bitcast.58) | data formatting | bytes 8388608 | tf_op jit(solution)/shard_map/reshape | solution.py:34
  145.8 2.6 %fusion = bf16[64,128,128]{2,1,0:T(8,128)(2,1)S(1)} fusion(f32[8,128,8,128]{3,1,2,0:T(8,128)} %copy.48, f32[64]{0:T(128)S(1)} %convert_element_type.70), kind=kLoop, calls=%fused_computation.6 | loop fusion | flops 2097152 | bytes 6291712 | tf_op jit(solution)/shard_map/convert_element_type | solution.py:111
  148.4 2.2 gather_fusion.3
  150.6 3.2 %broadcast_select_fusion.1 = bf16[64,128,128]{2,1,0:T(8,128)(2,1)} fusion(bf16[64,128,128]{2,1,0:T(8,128)(2,1)} %gather_fusion.3, pred[64]{0:T(512)(128)(4,1)S(1)} %get-tuple-element.15), kind=kLoop, calls=%fused_computation.24 | loop fusion | flops 1048576 | bytes 4194368 | tf_op jit(solution)/shard_map/jit(_take)/select_n | solution.py:111
  153.8 3.6 %all-to-all-start.2 = ((bf16[64,128,128]{2,1,0:T(8,128)(2,1)}), bf16[64,128,128]{2,1,0:T(8,128)(2,1)S(1)}, u32[]{:S(2)}, u32[]{:S(2)}) async-start(bf16[64,128,128]{2,1,0:T(8,128)(2,1)} %broadcast_select_fusion.1), calls=%async_computation.2 | async-start | bytes 4194304 | tf_op jit(solution)/shard_map/all_to_all | solution.py:103
  157.5 24.9 %all-to-all-done.2 = bf16[64,128,128]{2,1,0:T(8,128)(2,1)S(1)} async-done(((bf16[64,128,128]{2,1,0:T(8,128)(2,1)}), bf16[64,128,128]{2,1,0:T(8,128)(2,1)S(1)}, u32[]{:S(2)}, u32[]{:S(2)}) %all-to-all-start.2) | async-done | bytes 2097184 | tf_op jit(solution)/shard_map/all_to_all | solution.py:103
  182.4 2.2 gather_fusion.4
  184.6 1.8 broadcast_select_fusion
  186.4 59.5 %all_to_all.20 = bf16[64,128,128]{2,1,0:T(8,128)(2,1)S(1)} all-to-all(bf16[64,128,128]{2,1,0:T(8,128)(2,1)S(1)} %broadcast_select_fusion), channel_id=1, replica_groups=mesh['row'=64,'col'=4] {'row'}, dimensions={0} | all-to-all | bytes 4194304 | tf_op jit(solution)/shard_map/all_to_all | solution.py:103
  (60 shorter events, 12.3 us)
Async XLA Ops:
  0.0 1.9 copy-start
  4.5 64.2 %all-to-all-start = ((bf16[64,128,128]{2,1,0:T(8,128)(2,1)}), bf16[64,128,128]{2,1,0:T(8,128)(2,1)S(1)}, u32[]{:S(2)}, u32[]{:S(2)}) async-start(bf16[64,128,128]{2,1,0:T(8,128)(2,1)} %broadcast_select_fusion.3), calls=%async_computation | async-start | bytes 4194304 | tf_op jit(solution)/shard_map/all_to_all | solution.py:103
  74.0 4.6 %copy-start.4 = (s32[1,8,8]{2,1,0:T(8,128)S(1)}, s32[1,8,8]{2,1,0:T(8,128)}, u32[]{:S(2)}) copy-start(s32[1,8,8]{2,1,0:T(8,128)} %param.8) | copy-start | bytes 772
  74.0 4.7 %copy-start.3 = (bf16[1024,128]{1,0:T(8,128)(2,1)S(1)}, bf16[1024,128]{1,0:T(8,128)(2,1)}, u32[]{:S(2)}) copy-start(bf16[1024,128]{1,0:T(8,128)(2,1)} %param.9) | copy-start | bytes 786436
  74.0 30.6 %all-to-all-start.1 = ((bf16[64,128,128]{2,1,0:T(8,128)(2,1)}), bf16[64,128,128]{2,1,0:T(8,128)(2,1)}, u32[]{:S(2)}, u32[]{:S(2)}) async-start(bf16[64,128,128]{2,1,0:T(8,128)(2,1)} %broadcast_select_fusion.2), calls=%async_computation.1 | async-start | bytes 4194304 | tf_op jit(solution)/shard_map/all_to_all | solution.py:103
  114.6 2.7 %copy-start.6 = (bf16[1024,1024]{1,0:T(8,128)(2,1)}, bf16[1024,1024]{1,0:T(8,128)(2,1)S(1)}, u32[]{:S(2)}) copy-start(bf16[1024,1024]{1,0:T(8,128)(2,1)S(1)} %fusion.12) | copy-start | bytes 6291460
  129.9 4.8 %copy-start.2 = (bf16[1024,896]{0,1:T(8,128)(2,1)S(1)}, bf16[1024,896]{0,1:T(8,128)(2,1)}, u32[]{:S(2)}) copy-start(bf16[1024,896]{0,1:T(8,128)(2,1)} %fusion.1) | copy-start | bytes 5505028
  129.9 4.9 %copy-start.5 = (f32[1024,1024]{0,1:T(8,128)S(1)}, f32[1024,1024]{0,1:T(8,128)}, u32[]{:S(2)}) copy-start(f32[1024,1024]{0,1:T(8,128)} %fusion.4) | copy-start | bytes 12582916
  129.9 4.9 %copy-start.7 = (bf16[1024,1024]{1,0:T(8,128)(2,1)S(1)}, bf16[1024,1024]{1,0:T(8,128)(2,1)}, u32[]{:S(2)}) copy-start(bf16[1024,1024]{1,0:T(8,128)(2,1)} %copy-done.6) | copy-start | bytes 6291460
  153.8 28.6 %all-to-all-start.2 = ((bf16[64,128,128]{2,1,0:T(8,128)(2,1)}), bf16[64,128,128]{2,1,0:T(8,128)(2,1)S(1)}, u32[]{:S(2)}, u32[]{:S(2)}) async-start(bf16[64,128,128]{2,1,0:T(8,128)(2,1)} %broadcast_select_fusion.1), calls=%async_computation.2 | async-start | bytes 4194304 | tf_op jit(solution)/shard_map/all_to_all | solution.py:103
  186.4 61.8 %copy-start.1 = (bf16[12,128,128]{2,1,0:T(8,128)(2,1)S(1)}, bf16[12,128,128]{2,1,0:T(8,128)(2,1)}, u32[]{:S(2)}) copy-start(bf16[12,128,128]{2,1,0:T(8,128)(2,1)} %param.6) | copy-start | bytes 1179652

commit v2 on v1

v2 whole, which is shorter than its diff:
```python
import functools

import jax
import jax.numpy as jnp
from jax import lax
from jax.experimental import pallas as pl
from jax.experimental.pallas import tpu as pltpu
from jax.sharding import Mesh
from jax.sharding import PartitionSpec as P


def dot(a, b):
    return jnp.dot(a, b, preferred_element_type=jnp.float32)


def adjoint_kernel(span, entry_ref, keep_ref, *refs):
    blocks, cot_ref, outs = refs[:4], refs[4], refs[5:9]
    x, square, iterate, left, right, grad_t, head, head_square, staged, arrived, sent = refs[9:]
    order, width = cot_ref.shape
    edge = order // width
    bf16, f32 = jnp.bfloat16, jnp.float32
    spans = [pl.ds(start, span) for start in range(0, order, span)]

    def at(index, size):
        return pl.ds(pl.multiple_of(index * size, size), size)

    def kept(block, entry):
        return block * keep_ref[entry].astype(f32).astype(bf16)

    room = staged.shape[1]
    arrivals = [
        pltpu.make_async_copy(block_ref, staged.at[source], arrived.at[source])
        for source, block_ref in enumerate(blocks)
    ]
    for copy in arrivals:
        copy.start()
    for source, copy in enumerate(arrivals):
        copy.wait()

        @pl.loop(0, room, unroll=4)
        def place(j, source=source):
            entry = entry_ref[source, j]
            x[at(entry // edge, width), at(entry % edge, width)] = kept(staged[source, j], entry)

    for c in spans:
        square[:, c] = dot(x[...], x[:, c]).astype(bf16)
    for c in spans:
        iterate[:, c] = (1.5 * x[:, c].astype(f32) - 0.5 * dot(x[...], square[:, c])).astype(bf16)

    one, two = width, 2 * width
    v, tail = 2 * two, 3 * two
    cot_t = cot_ref[...].astype(f32).T.astype(bf16)
    pulled_t = dot(cot_t, iterate[...]).astype(bf16)
    right[v : v + one, :] = pulled_t
    right[v + one : v + two, :] = cot_t
    left[:, :one] = iterate[:, :one]
    left[:, one:two] = dot(iterate[...], iterate[:, :one]).astype(bf16)
    left[:, tail : tail + one] = x[:, :one]
    left[:, tail + one :] = square[:, :one]
    head[...] = 1.5 * cot_t.astype(f32) - 0.5 * dot(pulled_t, iterate[...])
    right[tail + one :, :] = (-2.0 * head[...]).astype(bf16)
    rows = jnp.concatenate([right[v : v + two, :], right[tail + one :, :]])
    for c in spans:
        onto_x = dot(rows, x[:, c])
        right[two:v, c] = onto_x[:two].astype(bf16)
        right[tail : tail + one, c] = onto_x[two:].astype(bf16)
        onto_square = dot(rows, square[:, c])
        right[:two, c] = onto_square[:two].astype(bf16)
        head_square[:, c] = onto_square[two:]
    w = left[:, :two]
    left[:, two:v] = dot(x[...], w).astype(bf16)
    left[:, v:tail] = dot(square[...], w).astype(bf16)

    for c in spans:
        cot = -0.5 * dot(left[:, :two], right[v : v + two, c])
        rest = 0.25 * dot(left[...], right[:, c])
        top = (cot[:one] + head[:, c]).astype(bf16).astype(f32)
        grad_t[:one, c] = (1.5 * top + rest[:one] + 0.25 * head_square[:, c]).astype(bf16)
        grad_t[one:, c] = (1.5 * cot[one:].astype(bf16).astype(f32) + rest[one:]).astype(bf16)

    departures = []
    for target, out_ref in enumerate(outs):

        @pl.loop(0, room, unroll=4)
        def send(j, target=target):
            entry = entry_ref[len(blocks) + target, j]
            block = grad_t[at(entry % edge, width), at(entry // edge, width)]
            staged[target, j] = kept(block, entry)

        departures.append(pltpu.make_async_copy(staged.at[target], out_ref, sent.at[target]))
        departures[-1].start()
    for copy in departures:
        copy.wait()


def adjoint_pieces(entry, keep, blocks, cot, span=512):
    order, width = cot.shape
    room = blocks[0].shape[0]
    vmem = pl.BlockSpec(memory_space=pltpu.VMEM)
    anywhere = pl.BlockSpec(memory_space=pl.ANY)
    smem = pl.BlockSpec(memory_space=pltpu.SMEM)
    whole = pltpu.VMEM((order, order), jnp.bfloat16)
    strip = pltpu.VMEM((width, order), jnp.float32)
    return pl.pallas_call(
        functools.partial(adjoint_kernel, span),
        out_shape=[jax.ShapeDtypeStruct((room, width, width), jnp.bfloat16)] * 4,
        in_specs=[smem, smem] + [anywhere] * 4 + [vmem],
        out_specs=[anywhere] * 4,
        scratch_shapes=[whole] * 6
        + [strip] * 2
        + [pltpu.VMEM((4, room, width, width), jnp.bfloat16)]
        + [pltpu.SemaphoreType.DMA((4,))] * 2,
        compiler_params=pltpu.CompilerParams(vmem_limit_bytes=40 << 20),
        cost_estimate=pl.CostEstimate(flops=11_000_000_000, bytes_accessed=5 << 20, transcendentals=0),
    )(entry, keep, *blocks, cot)


def arrange(index, sources, counts):
    split = len(sources) == 1
    fixed = counts if split else [source.shape[0] for source in sources]
    given, total = sum(source.shape[0] for source in sources), sum(counts)

    def kernel(index_ref, *refs):
        ins, outs = refs[: len(sources)], refs[len(sources) : len(sources) + len(counts)]
        came, leaves, arrived, sent = refs[len(sources) + len(counts) :]

        def bulk(ref, place, staged, start, done, inward):
            part = staged.at[pl.ds(start, ref.shape[0])]
            pair = (ref, part) if inward else (part, ref)
            return pltpu.make_async_copy(*pair, done.at[place])

        def starts(refs):
            return [sum(ref.shape[0] for ref in refs[:place]) for place in range(len(refs))]

        arrivals = [bulk(ref, i, came, s, arrived, True) for i, (ref, s) in enumerate(zip(ins, starts(ins)))]
        departures = [bulk(ref, i, leaves, s, sent, False) for i, (ref, s) in enumerate(zip(outs, starts(outs)))]
        for copy in arrivals:
            copy.start()
        start = 0
        for place, count in enumerate(fixed):
            if place < len(arrivals):
                arrivals[place].wait()

            @pl.loop(0, count, unroll=4)
            def _(j, start=start):
                spot = index_ref[start + j]
                if split:
                    leaves[start + j] = came[spot]
                else:
                    leaves[spot] = came[start + j]

            start += count
            if split:
                departures[place].start()
        if not split:
            departures[0].start()
        for copy in departures:
            copy.wait()

    anywhere = pl.BlockSpec(memory_space=pl.ANY)
    shape, dtype = sources[0].shape[1:], sources[0].dtype
    return pl.pallas_call(
        kernel,
        out_shape=[jax.ShapeDtypeStruct((count, *shape), dtype) for count in counts],
        in_specs=[pl.BlockSpec(memory_space=pltpu.SMEM)] + [anywhere] * len(sources),
        out_specs=[anywhere] * len(counts),
        scratch_shapes=[pltpu.VMEM((given, *shape), dtype), pltpu.VMEM((total, *shape), dtype)]
        + [pltpu.SemaphoreType.DMA((len(sources),)), pltpu.SemaphoreType.DMA((len(counts),))],
        compiler_params=pltpu.CompilerParams(vmem_limit_bytes=16 << 20),
        cost_estimate=pl.CostEstimate(flops=0, bytes_accessed=4 << 20, transcendentals=0),
    )(index, *sources)


AXES = ("x", "z", "core", "y")
SIZES = dict(x=4, z=8, core=2, y=4)


def shift(blocks, axis, step):
    count = SIZES[axis]
    return lax.ppermute(blocks, axis, [(i, (i + step) % count) for i in range(count)])


def picked_sum(hits, values):
    return jnp.sum(jnp.where(hits, values, 0), axis=-1)


def tables(block_ids, slot_count):
    nx, nz, nk, ny = (SIZES[a] for a in AXES)
    mx, mz, mk, my = (lax.axis_index(a) for a in AXES)
    entries = block_ids.shape[1]
    room = entries // ny
    by_place = block_ids.reshape(nx, nz, nk, ny * entries)
    level = lax.dynamic_index_in_dim(by_place, mz, 1, keepdims=False)
    owner, slot = level // slot_count, level % slot_count
    oy, ok, oz, ox = owner % ny, owner // ny % nk, owner // (ny * nk) % nz, owner // (ny * nk * nz)
    asked = (ox == mx) & (ok == mk) & (oy == my)
    far = jnp.where(asked, (oz - mz) % nz, nz)
    slots = picked_sum(far[:, :, None, :] == jnp.arange(nz)[:, None], slot[:, :, None, :])
    slots = jnp.roll(jnp.roll(slots, -mx, axis=0), -mk, axis=1)

    def mine(a):
        a = lax.dynamic_index_in_dim(a, mx, 0, keepdims=False)
        return lax.dynamic_index_in_dim(a, mk, 0, keepdims=False).reshape(ny, entries)

    oy, ok, oz, ox = mine(oy), mine(ok), mine(oz), mine(ox)
    stand = (((ok - mk) % nk) * nx + (mx - ox) % nx) * nz + (oz - mz) % nz
    stand = jnp.roll(stand, -my, axis=0)
    here = jnp.roll(oy == my, -my, axis=0)
    rank = jnp.cumsum(here.astype(jnp.int32), axis=1) - 1
    rank = jnp.where(here, rank, room)
    place = picked_sum(rank[:, None, :] == jnp.arange(room)[:, None], stand[:, None, :])
    mine_y = lax.dynamic_index_in_dim(oy, my, 0, keepdims=False)
    there = (mine_y[None, :] - my) % ny == jnp.arange(ny)[:, None]
    rank = jnp.cumsum(there.astype(jnp.int32), axis=1) - 1
    rank = jnp.where(there, rank, room)
    entry = picked_sum(rank[:, None, :] == jnp.arange(room)[:, None], jnp.arange(entries))
    return slots, place, entry


def shards(h_blocks, block_ids, pattern, result_grad):
    nx, nz, nk, ny = (SIZES[a] for a in AXES)
    slot_count, width, _ = h_blocks.shape
    entries = block_ids.shape[1]
    room = entries // ny
    slots, place, entry = tables(block_ids, slot_count)

    mx, mz, mk = (lax.axis_index(a) for a in AXES[:3])

    def over_row(blocks):
        return lax.all_to_all(blocks, AXES[:3], split_axis=0, concat_axis=0, tiled=True)

    level_x, level_z, level_k = jnp.meshgrid(jnp.arange(nx), jnp.arange(nz), jnp.arange(nk), indexing="ij")
    stand = ((((level_k - mk) % nk) * nx + (mx - level_x) % nx) * nz + (level_z - mz) % nz).reshape(-1)
    mine = block_ids // slot_count == (lax.axis_index(AXES[:3]) * ny + lax.axis_index("y"))
    asked = jnp.sum(jnp.where(mine, block_ids % slot_count, 0).reshape(entries, -1), axis=1)
    row_of_stand = picked_sum(stand[None, :] == jnp.arange(entries)[:, None], jnp.arange(entries))
    place = picked_sum(
        place.reshape(-1)[:, None] == jnp.arange(entries), row_of_stand
    ).reshape(place.shape)
    (asked_blocks,) = arrange(asked, [h_blocks], [entries])
    held = over_row(asked_blocks)

    order = jnp.concatenate([place[1], place[3], place[2], place[0]])
    ahead, behind, across, own = arrange(order, [held], [room] * ny)
    near, back, far = shift(ahead, "y", 1), shift(behind, "y", -1), shift(across, "y", 2)
    turned = jnp.stack([entry[i] for i in (0, 3, 1, 2, 1, 3, 2, 0)])
    ahead, behind, across, own = adjoint_pieces(
        turned, pattern.reshape(-1), [own, near, back, far], result_grad
    )
    near, back, far = shift(ahead, "y", 1), shift(behind, "y", -1), shift(across, "y", 2)
    order = jnp.concatenate([place[3], place[1], place[2], place[0]])
    (held,) = arrange(order, [near, back, far, own], [entries])

    held = over_row(held)
    weights = (asked[None, :] == jnp.arange(slot_count)[:, None]).astype(jnp.bfloat16)
    return jnp.einsum("sr,rab->sba", weights, held, preferred_element_type=jnp.float32)


def solution(mesh):
    torus = Mesh(mesh.devices.reshape([SIZES[a] for a in AXES]), AXES)
    in_specs = (P(AXES, None, None), P(), P(AXES, None, None), P(AXES, None))
    return jax.shard_map(
        shards, mesh=torus, in_specs=in_specs, out_specs=P(AXES, None, None), check_vma=False
    )
```

time: 249 us -> 200 us (0.80)
  matrix products: 24.7 us -> 1.23 us
  local copies, waits for them, and re-layouts: 24.3 us -> 5.05 us
  Pallas kernels: 0 us -> 18.1 us
  other arithmetic: 17.1 us -> 2.45 us
  waiting for transfers between devices: 101 us -> 91.8 us
    all_to_all x3 -> x1, waiting for transfers between devices: 101 us -> 48.5 us  [over_row(): lax.all_to_all(blocks, AXES[:3], split_axis=0, concat_axis=0, tiled=True)]
    ppermute x0 -> x6, waiting for transfers between devices: none -> 43.2 us  [shift(): lax.ppermute(blocks, axis, [(i, (i + step) % count) for i in range(count)])]
    dot_general x10 -> x1, matrix products: 24.7 us -> 1.23 us  [shards(): jnp.einsum('sr,rab->sba', weights, held, preferred_element_type=jnp.float32)]
    pallas_call x0 -> x4, Pallas kernels: none -> 18.1 us  [the longest x1 14.1 us: adjoint_pieces(): pl.pallas_call(functools.partial(adjoint_kernel, span), out_shape=[jax.Sh...]
    select_n x10 -> x2, other arithmetic: 10 us -> 0.02 us  [the longest x1 0.01 us: tables(): rank = jnp.where(here, rank, room)]
    gather x5 -> x0, local copies, waits for them, and re-layouts: 9.93 us -> none  [the longest x1 2.54 us: shards(): fetched = jnp.take(arrived, spot, axis=0)]
    reshape x3, local copies, waits for them, and re-layouts: 8.88 us -> 0.27 us  [the longest x1 0.11 us: tables(): by_place = block_ids.reshape(nx, nz, nk, ny * entries)]
    all_to_all x3 -> x1, starting transfers between devices: 21.2 us -> 13.1 us  [over_row(): lax.all_to_all(blocks, AXES[:3], split_axis=0, concat_axis=0, tiled=True)]
  transfers between devices with their start and end apart: 3 -> 7, of which waited for: 3 -> 5; matrix products, arithmetic and copies ran while one was open for 0% -> 1% of each run, Pallas kernels for 0% -> 0%
where the time goes in v2:
time: 200 us
  waiting for transfers between devices  91.8 us (46%)
  blocking collectives  60.3 us (30%)
  starting transfers between devices  20.3 us (10%)
  Pallas kernels  18.1 us (9%)
  local copies, waits for them, and re-layouts  5.05 us (3%)
  other arithmetic  2.45 us (1%)
    all_to_all x1, blocking collectives, over_row(): lax.all_to_all(blocks, AXES[:3], split_axis=0, concat_axis=0, tiled=True)  60.3 us
    all_to_all x1, waiting for transfers between devices, over_row(): lax.all_to_all(blocks, AXES[:3], split_axis=0, concat_axis=0, tiled=True)  48.5 us
    ppermute x6, waiting for transfers between devices, shift(): lax.ppermute(blocks, axis, [(i, (i + step) % count) for i in range(count)])  43.2 us
    pallas_call x1, Pallas kernels, adjoint_pieces(): pl.pallas_call(functools.partial(adjoint_kernel, span), out_shape=[jax.Sh...  14.1 us
    all_to_all x1, starting transfers between devices, over_row(): lax.all_to_all(blocks, AXES[:3], split_axis=0, concat_axis=0, tiled=True)  13.1 us
    ppermute x6, starting transfers between devices, shift(): lax.ppermute(blocks, axis, [(i, (i + step) % count) for i in range(count)])  7.21 us
  transfers between devices with their start and end apart: 7, of which 5 were waited for; matrix products, arithmetic and copies ran while one was open for 1% of the time, Pallas kernels for 0%

profile of v2, /device:TPU:1, one launch (start us, length us, event | category | flops | bytes accessed | tf_op | source)
XLA Modules:
  0.0 199.5 jit_solution(11415500240784216225)
XLA Ops:
  0.0 0.9 fusion.7
  1.2 1.0 copy-done.1
  2.2 1.1 shard_map.46
  3.3 1.3 copy-done
  4.6 13.1 %all-to-all-start = ((bf16[64,128,128]{2,1,0:T(8,128)(2,1)}), bf16[64,128,128]{2,1,0:T(8,128)(2,1)S(1)}, u32[]{:S(2)}, u32[]{:S(2)}) async-start(bf16[64,128,128]{2,1,0:T(8,128)(2,1)} %copy-done), calls=%async_computation | async-start | bytes 4194304 | tf_op jit(solution)/shard_map/all_to_all | solution.py:230
  18.3 0.2 reduce_window_sum.17
  19.8 0.2 select_reduce_fusion.1
  20.1 0.2 reduce_window_sum.18
  20.5 48.5 %all-to-all-done.refs_0_ = bf16[64,128,128]{2,1,0:T(8,128)(2,1)S(1)} async-done(((bf16[64,128,128]{2,1,0:T(8,128)(2,1)}), bf16[64,128,128]{2,1,0:T(8,128)(2,1)S(1)}, u32[]{:S(2)}, u32[]{:S(2)}) %all-to-all-start) | async-done | bytes 2097184 | tf_op jit(solution)/shard_map/all_to_all | solution.py:230
  69.0 1.7 shard_map.47
  70.8 1.4 collective-permute-start
  72.1 1.5 collective-permute-start.1
  73.7 1.6 collective-permute-start.2
  75.5 10.0 %collective-permute-done.refs_1_ = bf16[16,128,128]{2,1,0:T(8,128)(2,1)S(1)} collective-permute-done((bf16[16,128,128]{2,1,0:T(8,128)(2,1)}, bf16[16,128,128]{2,1,0:T(8,128)(2,1)S(1)}, u32[]{:S(2)}, u32[]{:S(2)}) %collective-permute-start) | collective-permute-done | bytes 524320 | tf_op jit(solution)/shard_map/ppermute | solution.py:180
  85.5 12.3 %collective-permute-done.2.refs_3_ = bf16[16,128,128]{2,1,0:T(8,128)(2,1)S(1)} collective-permute-done((bf16[16,128,128]{2,1,0:T(8,128)(2,1)S(1)}, bf16[16,128,128]{2,1,0:T(8,128)(2,1)S(1)}, u32[]{:S(2)}, u32[]{:S(2)}) %collective-permute-start.2) | collective-permute-done | bytes 524320 | tf_op jit(solution)/shard_map/ppermute | solution.py:180
  97.9 14.1 %shard_map.48 = (bf16[16,128,128]{2,1,0:T(8,128)(2,1)S(1)}, bf16[16,128,128]{2,1,0:T(8,128)(2,1)S(1)}, bf16[16,128,128]{2,1,0:T(8,128)(2,1)S(1)}, bf16[16,128,128]{2,1,0:T(8,128)(2,1)S(1)}) custom-call(s32[8,16]{1,0:T(8,128)S(1)} %stack.3.entry_ref, s32[64]{0:T(128)S(1)} %reshape.172.keep_ref, bf16[16,128,128]{2,1,0:T(8,128)(2,1)S(1)} %get-tuple-element.13.refs_0_, ...), custom_call_target="tpu_custom_call" | custom-call | flops 11000000512 | bytes 5242880 | tf_op jit(solution)/shard_map/pallas_call | solution.py:104
  112.0 0.6 collective-permute-start.3
  112.6 2.1 %collective-permute-start.4 = (bf16[16,128,128]{2,1,0:T(8,128)(2,1)S(1)}, bf16[16,128,128]{2,1,0:T(8,128)(2,1)S(1)}, u32[]{:S(2)}, u32[]{:S(2)}) collective-permute-start(bf16[16,128,128]{2,1,0:T(8,128)(2,1)S(1)} %get-tuple-element.18), channel_id=1, source_target_pairs={{0,3},{1,0},{2,1},{3,2},{4,7},{5,4},{6,5},{7,6},{8,11},{9,8},{10,9... | collective-permute-start | bytes 1572872 | tf_op jit(solution)/shard_map/ppermute | solution.py:180
  114.7 11.8 %collective-permute-done.3.refs_0_ = bf16[16,128,128]{2,1,0:T(8,128)(2,1)S(1)} collective-permute-done((bf16[16,128,128]{2,1,0:T(8,128)(2,1)S(1)}, bf16[16,128,128]{2,1,0:T(8,128)(2,1)S(1)}, u32[]{:S(2)}, u32[]{:S(2)}) %collective-permute-start.3) | collective-permute-done | bytes 524320 | tf_op jit(solution)/shard_map/ppermute | solution.py:180
  126.6 9.0 %collective-permute-done.5.refs_2_ = bf16[16,128,128]{2,1,0:T(8,128)(2,1)S(1)} collective-permute-done((bf16[16,128,128]{2,1,0:T(8,128)(2,1)S(1)}, bf16[16,128,128]{2,1,0:T(8,128)(2,1)S(1)}, u32[]{:S(2)}, u32[]{:S(2)}) %collective-permute-start.5) | collective-permute-done | bytes 524320 | tf_op jit(solution)/shard_map/ppermute | solution.py:180
  135.6 1.1 shard_map.49
  136.7 60.3 %all_to_all.10 = bf16[64,128,128]{2,1,0:T(8,128)(2,1)S(1)} all-to-all(bf16[64,128,128]{2,1,0:T(8,128)(2,1)S(1)} %shard_map.49), channel_id=1, replica_groups=mesh['x'=4,'z'=8,'core'=2,'y'=4] {'x','z','core'}, dimensions={0} | all-to-all | bytes 4194304 | tf_op jit(solution)/shard_map/all_to_all | solution.py:230
  197.1 1.2 fusion.2
  198.3 1.2 copy.22
  (56 shorter events, 2.3 us)
Async XLA Ops:
  1.1 1.0 copy-start.1
  3.3 1.4 copy-start
  4.6 13.2 %copy-start.3 = (s32[256,64]{0,1:T(8,128)S(1)}, s32[256,64]{0,1:T(8,128)}, u32[]{:S(2)}) copy-start(s32[256,64]{0,1:T(8,128)} %param.5) | copy-start | bytes 196612
  4.6 64.4 %all-to-all-start = ((bf16[64,128,128]{2,1,0:T(8,128)(2,1)}), bf16[64,128,128]{2,1,0:T(8,128)(2,1)S(1)}, u32[]{:S(2)}, u32[]{:S(2)}) async-start(bf16[64,128,128]{2,1,0:T(8,128)(2,1)} %copy-done), calls=%async_computation | async-start | bytes 4194304 | tf_op jit(solution)/shard_map/all_to_all | solution.py:230
  17.8 57.6 %copy-start.4 = (s32[1,8,8]{2,1,0:T(8,128)S(1)}, s32[1,8,8]{2,1,0:T(8,128)}, u32[]{:S(2)}) copy-start(s32[1,8,8]{2,1,0:T(8,128)} %param.6) | copy-start | bytes 772
  17.8 80.1 %copy-start.2 = (bf16[1024,128]{1,0:T(8,128)(2,1)S(1)}, bf16[1024,128]{1,0:T(8,128)(2,1)}, u32[]{:S(2)}) copy-start(bf16[1024,128]{1,0:T(8,128)(2,1)} %refs_4_.1) | copy-start | bytes 786436
  70.8 14.7 %collective-permute-start = (bf16[16,128,128]{2,1,0:T(8,128)(2,1)}, bf16[16,128,128]{2,1,0:T(8,128)(2,1)S(1)}, u32[]{:S(2)}, u32[]{:S(2)}) collective-permute-start(bf16[16,128,128]{2,1,0:T(8,128)(2,1)} %get-tuple-element.14), channel_id=1, source_target_pairs={{0,1},{1,2},{2,3},{3,0},{4,5},{5,6},{6,7},{7,4},{8,9},{9,10},{10,1... | collective-permute-start | bytes 1572872 | tf_op jit(solution)/shard_map/ppermute | solution.py:180
  72.1 13.4 %collective-permute-start.1 = (bf16[16,128,128]{2,1,0:T(8,128)(2,1)}, bf16[16,128,128]{2,1,0:T(8,128)(2,1)S(1)}, u32[]{:S(2)}, u32[]{:S(2)}) collective-permute-start(bf16[16,128,128]{2,1,0:T(8,128)(2,1)} %get-tuple-element.15), channel_id=1, source_target_pairs={{0,3},{1,0},{2,1},{3,2},{4,7},{5,4},{6,5},{7,6},{8,11},{9,8},{10,9... | collective-permute-start | bytes 1572872 | tf_op jit(solution)/shard_map/ppermute | solution.py:180
  73.7 24.2 %collective-permute-start.2 = (bf16[16,128,128]{2,1,0:T(8,128)(2,1)S(1)}, bf16[16,128,128]{2,1,0:T(8,128)(2,1)S(1)}, u32[]{:S(2)}, u32[]{:S(2)}) collective-permute-start(bf16[16,128,128]{2,1,0:T(8,128)(2,1)S(1)} %get-tuple-element.16), channel_id=1, source_target_pairs={{0,2},{1,3},{2,0},{3,1},{4,6},{5,7},{6,4},{7,5},{8,10},{9,11},{10,... | collective-permute-start | bytes 1572872 | tf_op jit(solution)/shard_map/ppermute | solution.py:180
  112.0 14.6 %collective-permute-start.3 = (bf16[16,128,128]{2,1,0:T(8,128)(2,1)S(1)}, bf16[16,128,128]{2,1,0:T(8,128)(2,1)S(1)}, u32[]{:S(2)}, u32[]{:S(2)}) collective-permute-start(bf16[16,128,128]{2,1,0:T(8,128)(2,1)S(1)} %get-tuple-element.17), channel_id=1, source_target_pairs={{0,1},{1,2},{2,3},{3,0},{4,5},{5,6},{6,7},{7,4},{8,9},{9,10},{10,1... | collective-permute-start | bytes 1572872 | tf_op jit(solution)/shard_map/ppermute | solution.py:180
  112.6 14.0 %collective-permute-start.4 = (bf16[16,128,128]{2,1,0:T(8,128)(2,1)S(1)}, bf16[16,128,128]{2,1,0:T(8,128)(2,1)S(1)}, u32[]{:S(2)}, u32[]{:S(2)}) collective-permute-start(bf16[16,128,128]{2,1,0:T(8,128)(2,1)S(1)} %get-tuple-element.18), channel_id=1, source_target_pairs={{0,3},{1,0},{2,1},{3,2},{4,7},{5,4},{6,5},{7,6},{8,11},{9,8},{10,9... | collective-permute-start | bytes 1572872 | tf_op jit(solution)/shard_map/ppermute | solution.py:180
  114.7 20.9 %collective-permute-start.5 = (bf16[16,128,128]{2,1,0:T(8,128)(2,1)S(1)}, bf16[16,128,128]{2,1,0:T(8,128)(2,1)S(1)}, u32[]{:S(2)}, u32[]{:S(2)}) collective-permute-start(bf16[16,128,128]{2,1,0:T(8,128)(2,1)S(1)} %get-tuple-element.19), channel_id=1, source_target_pairs={{0,2},{1,3},{2,0},{3,1},{4,6},{5,7},{6,4},{7,5},{8,10},{9,11},{10,... | collective-permute-start | bytes 1572872 | tf_op jit(solution)/shard_map/ppermute | solution.py:180

commit v3 on v2

v3 whole, which is shorter than its diff:
```python
import functools

import jax
import jax.numpy as jnp
from jax import lax
from jax.experimental import pallas as pl
from jax.experimental.pallas import tpu as pltpu
from jax.sharding import Mesh
from jax.sharding import PartitionSpec as P


def dot(a, b):
    return jnp.dot(a, b, preferred_element_type=jnp.float32)


def starts_of(refs):
    sizes = [ref.shape[0] for ref in refs]
    return [sum(sizes[:place]) for place in range(len(sizes))]


def bulk(refs, staged, done, inward):
    copies = []
    for place, (ref, start) in enumerate(zip(refs, starts_of(refs))):
        part = staged.at[pl.ds(start, ref.shape[0])]
        pair = (ref, part) if inward else (part, ref)
        copies.append(pltpu.make_async_copy(*pair, done.at[place]))
    return copies


def adjoint_kernel(span, arrays, entry_ref, keep_ref, *refs):
    blocks, cot_ref, outs = refs[:arrays], refs[arrays], refs[arrays + 1 : 2 * arrays + 1]
    x, square, iterate, left, right, grad_t, head, head_square, staged, arrived, sent = refs[
        2 * arrays + 1 :
    ]
    order, width = cot_ref.shape
    edge = order // width
    bf16, f32 = jnp.bfloat16, jnp.float32
    spans = [pl.ds(start, span) for start in range(0, order, span)]

    def at(index, size):
        return pl.ds(pl.multiple_of(index * size, size), size)

    def kept(block, entry):
        return block * keep_ref[entry].astype(f32).astype(bf16)

    arrivals = bulk(blocks, staged, arrived, True)
    for copy in arrivals:
        copy.start()
    for copy, ref, start in zip(arrivals, blocks, starts_of(blocks)):
        copy.wait()

        @pl.loop(start, start + ref.shape[0], unroll=4)
        def place(j):
            entry = entry_ref[0, j]
            x[at(entry // edge, width), at(entry % edge, width)] = kept(staged[j], entry)

    for c in spans:
        square[:, c] = dot(x[...], x[:, c]).astype(bf16)
    for c in spans:
        iterate[:, c] = (1.5 * x[:, c].astype(f32) - 0.5 * dot(x[...], square[:, c])).astype(bf16)

    one, two = width, 2 * width
    v, tail = 2 * two, 3 * two
    cot_t = cot_ref[...].astype(f32).T.astype(bf16)
    pulled_t = dot(cot_t, iterate[...]).astype(bf16)
    right[v : v + one, :] = pulled_t
    right[v + one : v + two, :] = cot_t
    left[:, :one] = iterate[:, :one]
    left[:, one:two] = dot(iterate[...], iterate[:, :one]).astype(bf16)
    left[:, tail : tail + one] = x[:, :one]
    left[:, tail + one :] = square[:, :one]
    head[...] = 1.5 * cot_t.astype(f32) - 0.5 * dot(pulled_t, iterate[...])
    right[tail + one :, :] = (-2.0 * head[...]).astype(bf16)
    rows = jnp.concatenate([right[v : v + two, :], right[tail + one :, :]])
    for c in spans:
        onto_x = dot(rows, x[:, c])
        right[two:v, c] = onto_x[:two].astype(bf16)
        right[tail : tail + one, c] = onto_x[two:].astype(bf16)
        onto_square = dot(rows, square[:, c])
        right[:two, c] = onto_square[:two].astype(bf16)
        head_square[:, c] = onto_square[two:]
    w = left[:, :two]
    left[:, two:v] = dot(x[...], w).astype(bf16)
    left[:, v:tail] = dot(square[...], w).astype(bf16)

    for c in spans:
        cot = -0.5 * dot(left[:, :two], right[v : v + two, c])
        rest = 0.25 * dot(left[...], right[:, c])
        top = (cot[:one] + head[:, c]).astype(bf16).astype(f32)
        grad_t[:one, c] = (1.5 * top + rest[:one] + 0.25 * head_square[:, c]).astype(bf16)
        grad_t[one:, c] = (1.5 * cot[one:].astype(bf16).astype(f32) + rest[one:]).astype(bf16)

    departures = bulk(outs, staged, sent, False)
    for copy, ref, start in zip(departures, outs, starts_of(outs)):

        @pl.loop(start, start + ref.shape[0], unroll=4)
        def send(j):
            entry = entry_ref[1, j]
            block = grad_t[at(entry % edge, width), at(entry // edge, width)]
            staged[j] = kept(block, entry)

        copy.start()
    for copy in departures:
        copy.wait()


def adjoint_pieces(entry, keep, blocks, cot, counts, span=512):
    order, width = cot.shape
    arrays = len(blocks)
    anywhere = pl.BlockSpec(memory_space=pl.ANY)
    smem = pl.BlockSpec(memory_space=pltpu.SMEM)
    whole = pltpu.VMEM((order, order), jnp.bfloat16)
    strip = pltpu.VMEM((width, order), jnp.float32)
    return pl.pallas_call(
        functools.partial(adjoint_kernel, span, arrays),
        out_shape=[jax.ShapeDtypeStruct((count, width, width), jnp.bfloat16) for count in counts],
        in_specs=[smem, smem] + [anywhere] * arrays + [pl.BlockSpec(memory_space=pltpu.VMEM)],
        out_specs=[anywhere] * arrays,
        scratch_shapes=[whole] * 6
        + [strip] * 2
        + [pltpu.VMEM((sum(counts), width, width), jnp.bfloat16)]
        + [pltpu.SemaphoreType.DMA((arrays,))] * 2,
        compiler_params=pltpu.CompilerParams(vmem_limit_bytes=40 << 20),
        cost_estimate=pl.CostEstimate(flops=11_000_000_000, bytes_accessed=5 << 20, transcendentals=0),
    )(entry, keep, *blocks, cot)


def arrange(index, sources, counts, into_source_order=False, outside=pl.ANY):
    given, total = sum(source.shape[0] for source in sources), sum(counts)

    def kernel(index_ref, *refs):
        ins, outs = refs[: len(sources)], refs[len(sources) : len(sources) + len(counts)]
        came, leaves, arrived, sent = refs[len(sources) + len(counts) :]
        arrivals = bulk(ins, came, arrived, True)
        departures = bulk(outs, leaves, sent, False)
        for copy in arrivals:
            copy.start()
        if into_source_order:
            for copy, ref, start in zip(arrivals, ins, starts_of(ins)):
                copy.wait()

                @pl.loop(start, start + ref.shape[0], unroll=4)
                def _(j):
                    leaves[index_ref[j]] = came[j]

            departures[0].start()
        else:
            for copy in arrivals:
                copy.wait()
            for copy, ref, start in zip(departures, outs, starts_of(outs)):

                @pl.loop(start, start + ref.shape[0], unroll=4 if ref.shape[0] % 4 == 0 else 2)
                def _(j):
                    leaves[j] = came[index_ref[j]]

                copy.start()
        for copy in departures:
            copy.wait()

    shape, dtype = sources[0].shape[1:], sources[0].dtype
    return pl.pallas_call(
        kernel,
        out_shape=[jax.ShapeDtypeStruct((count, *shape), dtype) for count in counts],
        in_specs=[pl.BlockSpec(memory_space=pltpu.SMEM)]
        + [pl.BlockSpec(memory_space=outside)] * len(sources),
        out_specs=[pl.BlockSpec(memory_space=outside)] * len(counts),
        scratch_shapes=[pltpu.VMEM((given, *shape), dtype), pltpu.VMEM((total, *shape), dtype)]
        + [pltpu.SemaphoreType.DMA((len(sources),)), pltpu.SemaphoreType.DMA((len(counts),))],
        compiler_params=pltpu.CompilerParams(vmem_limit_bytes=16 << 20),
        cost_estimate=pl.CostEstimate(flops=0, bytes_accessed=4 << 20, transcendentals=0),
    )(index, *sources)


AXES = ("x", "z", "core", "y")
SIZES = dict(x=4, z=8, core=2, y=4)
FIRST_LATE, LATE = 3, 3


def shift(blocks, axis, step):
    count = SIZES[axis]
    return lax.ppermute(blocks, axis, [(i, (i + step) % count) for i in range(count)])


def picked_sum(hits, values):
    return jnp.sum(jnp.where(hits, values, 0), axis=-1)


def tables(block_ids, slot_count):
    nx, nz, nk, ny = (SIZES[a] for a in AXES)
    mx, mz, mk, my = (lax.axis_index(a) for a in AXES)
    entries = block_ids.shape[1]
    room = entries // ny
    owners = block_ids // slot_count
    mine = owners == ((mx * nz + mz) * nk + mk) * ny + my
    asked = jnp.sum(jnp.where(mine, block_ids % slot_count, 0).reshape(nx * nz * nk, -1), axis=1)
    by_place = block_ids.reshape(nx, nz, nk, ny * entries)
    level = lax.dynamic_index_in_dim(by_place, mz, 1, keepdims=False)
    owner, slot = level // slot_count, level % slot_count
    row, oy = owner // ny, owner % ny
    ok, oz, ox = row % nk, row // nk % nz, row // (nk * nz)
    far = jnp.where((ox == mx) & (ok == mk) & (oy == my), (oz - mz) % nz, nz)
    slots = picked_sum(far[:, :, None, :] == jnp.arange(nz)[:, None], slot[:, :, None, :])
    slots = jnp.roll(jnp.roll(slots, -mx, axis=0), -mk, axis=1)

    def of_my_row(a):
        a = lax.dynamic_index_in_dim(a, mx, 0, keepdims=False)
        return lax.dynamic_index_in_dim(a, mk, 0, keepdims=False).reshape(ny, entries)

    row, oy, ok, oz, ox = (of_my_row(a) for a in (row, oy, ok, oz, ox))
    dk, dz, dx = (ok - mk) % nk, (oz - mz) % nz, (mx - ox) % nx
    late = (dz >= FIRST_LATE) & (dz < FIRST_LATE + LATE)
    early = nz - LATE
    group = jnp.where(late, LATE, early)
    within = jnp.where(dz < FIRST_LATE, dz, jnp.where(late, dz - FIRST_LATE, dz - LATE))
    stand = jnp.where(late, (nk + 1) * nx * early, 0) + within
    lane = jnp.where(dx == 0, 3, jnp.where(dx == 1, 0, jnp.where(dx == 3, 1, 2)))
    stand = stand + jnp.where(dk == 0, lane * nk, nk * nx + lane) * group
    here = oy == my
    rank = jnp.where(here, jnp.cumsum(here.astype(jnp.int32), axis=1) - 1, room)
    hits = rank[:, None, :] == jnp.arange(room)[:, None]
    ring = jnp.roll(picked_sum(hits, stand[:, None, :]), -my, axis=0)
    rows = jnp.roll(picked_sum(hits, row[:, None, :]), -my, axis=0)
    mine_y = lax.dynamic_index_in_dim(oy, my, 0, keepdims=False)
    there = (mine_y[None, :] - my) % ny == jnp.arange(ny)[:, None]
    rank = jnp.where(there, jnp.cumsum(there.astype(jnp.int32), axis=1) - 1, room)
    entry = picked_sum(rank[:, None, :] == jnp.arange(room)[:, None], jnp.arange(entries))
    return slots, asked, ring, rows, entry


def shards(h_blocks, block_ids, pattern, result_grad):
    nx, nz, nk, ny = (SIZES[a] for a in AXES)
    slot_count, width, _ = h_blocks.shape
    entries = block_ids.shape[1]
    room = entries // ny
    slots, asked, ring, rows, entry = tables(block_ids, slot_count)

    half = slot_count // 2
    up, down = [h_blocks], [h_blocks]
    for _ in range(nz // 2 - 1):
        up.append(shift(up[-1], "z", 1))
        down.append(shift(down[-1], "z", -1))
    up.append(shift(up[-1][:half], "z", 1))
    down.append(shift(down[-1][half:], "z", -1))
    early = [*down[:FIRST_LATE], up[2], up[1]]
    late = [down[3], up[4], down[4], up[3]]
    end = FIRST_LATE + LATE
    early_slots = jnp.concatenate([slots[:, :, :FIRST_LATE], slots[:, :, end:]], axis=2)

    def over_x_and_core(sources, wanted):
        size = wanted.shape[2]
        wanted = wanted + slot_count * jnp.arange(size)
        order = jnp.concatenate([wanted[i].reshape(-1) for i in (1, 3, 2, 0)])
        ahead, behind, across, own = arrange(order, sources, [nk * size] * nx)
        came = [shift(ahead, "x", 1), shift(behind, "x", -1), shift(across, "x", 2), own]
        other = jnp.concatenate([part[size:] for part in came])
        return [*came, shift(other, "core", 1)]

    held = over_x_and_core(early, early_slots)
    held = held + over_x_and_core(late, slots[:, :, FIRST_LATE:end])

    routes = [(step, room // 1) for step in (1, -1, 2) for _ in range(1)]
    counts = [count for _, count in routes] + [room]

    def over_col(parts):
        return [shift(part, "y", step) for part, (step, _) in zip(parts, routes)] + [parts[-1]]

    order = jnp.concatenate([ring[i] for i in (1, 3, 2, 0)])
    blocks = over_col(arrange(order, held, counts))
    came = jnp.concatenate([entry[i] for i in (3, 1, 2, 0)])
    leaves = jnp.concatenate([entry[i] for i in (1, 3, 2, 0)])
    pieces = adjoint_pieces(
        jnp.stack([came, leaves]), pattern.reshape(-1), blocks, result_grad, counts
    )
    order = jnp.concatenate([rows[i] for i in (3, 1, 2, 0)])
    (held,) = arrange(order, over_col(pieces), [entries], into_source_order=True)

    held = lax.all_to_all(held, AXES[:3], split_axis=0, concat_axis=0, tiled=True)
    weights = (asked[None, :] == jnp.arange(slot_count)[:, None]).astype(jnp.bfloat16)
    return jnp.einsum("sr,rab->sba", weights, held, preferred_element_type=jnp.float32)


def solution(mesh):
    torus = Mesh(mesh.devices.reshape([SIZES[a] for a in AXES]), AXES)
    in_specs = (P(AXES, None, None), P(), P(AXES, None, None), P(AXES, None))
    return jax.shard_map(
        shards, mesh=torus, in_specs=in_specs, out_specs=P(AXES, None, None), check_vma=False
    )
```

time: 200 us -> 197 us (0.985)
  blocking collectives: 60.3 us -> 0 us
  starting transfers between devices: 20.3 us -> 50.1 us
  waiting for transfers between devices: 91.8 us -> 113 us
  Pallas kernels: 18.1 us -> 24 us
    all_to_all x1 -> x0, blocking collectives: 60.3 us -> none  [over_row(): lax.all_to_all(blocks, AXES[:3], split_axis=0, concat_axis=0, tiled=True)]
    ppermute x6 -> x22, starting transfers between devices: 7.21 us -> 41.8 us  [shift(): lax.ppermute(blocks, axis, [(i, (i + step) % count) for i in range(count)])]
    ppermute x6 -> x22, waiting for transfers between devices: 43.2 us -> 61.6 us  [shift(): lax.ppermute(blocks, axis, [(i, (i + step) % count) for i in range(count)])]
    pallas_call x3 -> x4, Pallas kernels: 3.99 us -> 10 us  [arrange(): pl.pallas_call(kernel, out_shape=[jax.ShapeDtypeStruct((count, *shape), d...]
    all_to_all x1, starting transfers between devices: 13.1 us -> 8.27 us  [shards(): lax.all_to_all(held, AXES[:3], split_axis=0, concat_axis=0, tiled=True)]
    all_to_all x1, waiting for transfers between devices: 48.5 us -> 50.9 us  [shards(): lax.all_to_all(held, AXES[:3], split_axis=0, concat_axis=0, tiled=True)]
    concatenate x3 -> x10, other arithmetic: 0.1 us -> 2.1 us  [the longest x2 1.73 us: over_x_and_core(): other = jnp.concatenate([part[size:] for part in came])]
  transfers between devices with their start and end apart: 7 -> 23, of which waited for: 5 -> 10; matrix products, arithmetic and copies ran while one was open for 1% -> 3% of each run, Pallas kernels for 0% -> 2%
where the time goes in v3:
time: 197 us
  waiting for transfers between devices  113 us (57%)
  starting transfers between devices  50.1 us (25%)
  Pallas kernels  24 us (12%)
  local copies, waits for them, and re-layouts  4.81 us (2%)
  other arithmetic  3.82 us (2%)
    ppermute x22, waiting for transfers between devices, shift(): lax.ppermute(blocks, axis, [(i, (i + step) % count) for i in range(count)])  61.6 us
    all_to_all x1, waiting for transfers between devices, shards(): lax.all_to_all(held, AXES[:3], split_axis=0, concat_axis=0, tiled=True)  50.9 us
    ppermute x22, starting transfers between devices, shift(): lax.ppermute(blocks, axis, [(i, (i + step) % count) for i in range(count)])  41.8 us
    pallas_call x1, Pallas kernels, adjoint_pieces(): pl.pallas_call(functools.partial(adjoint_kernel, span, arrays), out_shape...  14 us
    pallas_call x4, Pallas kernels, arrange(): pl.pallas_call(kernel, out_shape=[jax.ShapeDtypeStruct((count, *shape), d...  10 us
    all_to_all x1, starting transfers between devices, shards(): lax.all_to_all(held, AXES[:3], split_axis=0, concat_axis=0, tiled=True)  8.27 us
  transfers between devices with their start and end apart: 23, of which 10 were waited for; matrix products, arithmetic and copies ran while one was open for 3% of the time, Pallas kernels for 2%

profile of v3, /device:TPU:1, one launch (start us, length us, event | category | flops | bytes accessed | tf_op | source)
XLA Modules:
  0.0 197.0 jit_solution(3826050903182328086)
XLA Ops:
  0.0 6.4 %collective-permute-start = (bf16[12,128,128]{2,1,0:T(8,128)(2,1)}, bf16[12,128,128]{2,1,0:T(8,128)(2,1)S(1)}, u32[]{:S(2)}, u32[]{:S(2)}) collective-permute-start(bf16[12,128,128]{2,1,0:T(8,128)(2,1)} %refs_0_.1), channel_id=1, source_target_pairs={{0,56},{8,0},{16,8},{24,16},{32,24},{40,32},{48,40},{56,48},{1,57}... | collective-permute-start | bytes 1179656 | tf_op jit(solution)/shard_map/ppermute | solution.py:181
  8.6 5.9 %collective-permute-done.refs_1_ = bf16[12,128,128]{2,1,0:T(8,128)(2,1)S(1)} collective-permute-done((bf16[12,128,128]{2,1,0:T(8,128)(2,1)}, bf16[12,128,128]{2,1,0:T(8,128)(2,1)S(1)}, u32[]{:S(2)}, u32[]{:S(2)}) %collective-permute-start) | collective-permute-done | bytes 393248 | tf_op jit(solution)/shard_map/ppermute | solution.py:181
  14.5 3.3 %collective-permute-start.1 = (bf16[12,128,128]{2,1,0:T(8,128)(2,1)S(1)}, bf16[12,128,128]{2,1,0:T(8,128)(2,1)S(1)}, u32[]{:S(2)}, u32[]{:S(2)}) collective-permute-start(bf16[12,128,128]{2,1,0:T(8,128)(2,1)S(1)} %collective-permute-done.refs_1_), channel_id=1, source_target_pairs={{0,56},{8,0},{16,8},{24,16},{32,24},{40,32},{48,40},{56,48},{1,57}... | collective-permute-start | bytes 1179656 | tf_op jit(solution)/shard_map/ppermute | solution.py:181
  19.1 5.6 %collective-permute-done.1.refs_2_ = bf16[12,128,128]{2,1,0:T(8,128)(2,1)S(1)} collective-permute-done((bf16[12,128,128]{2,1,0:T(8,128)(2,1)S(1)}, bf16[12,128,128]{2,1,0:T(8,128)(2,1)S(1)}, u32[]{:S(2)}, u32[]{:S(2)}) %collective-permute-start.1) | collective-permute-done | bytes 393248 | tf_op jit(solution)/shard_map/ppermute | solution.py:181
  24.7 3.4 %collective-permute-start.8 = (bf16[12,128,128]{2,1,0:T(8,128)(2,1)S(1)}, bf16[12,128,128]{2,1,0:T(8,128)(2,1)S(1)}, u32[]{:S(2)}, u32[]{:S(2)}) collective-permute-start(bf16[12,128,128]{2,1,0:T(8,128)(2,1)S(1)} %collective-permute-done.1.refs_2_), channel_id=1, source_target_pairs={{0,56},{8,0},{16,8},{24,16},{32,24},{40,32},{48,40},{56,48},{1,57}... | collective-permute-start | bytes 1179656 | tf_op jit(solution)/shard_map/ppermute | solution.py:181
  29.2 2.2 %shard_map.46 = (bf16[10,128,128]{2,1,0:T(8,128)(2,1)S(1)}, bf16[10,128,128]{2,1,0:T(8,128)(2,1)S(1)}, bf16[10,128,128]{2,1,0:T(8,128)(2,1)S(1)}, bf16[10,128,128]{2,1,0:T(8,128)(2,1)S(1)}) custom-call(s32[40]{0:T(128)S(1)} %pad_add_fusion.5.index_ref, bf16[12,128,128]{2,1,0:T(8,128)(2,1)S(1)} %copy-done, ...), custom_call_target="tpu_custom_call" | custom-call | bytes 4194304 | tf_op jit(solution)/shard_map/pallas_call | solution.py:161
  35.8 2.7 %collective-permute-start.11 = (bf16[6,128,128]{2,1,0:T(8,128)(2,1)S(1)}, bf16[6,128,128]{2,1,0:T(8,128)(2,1)S(1)}, u32[]{:S(2)}, u32[]{:S(2)}) collective-permute-start(bf16[6,128,128]{2,1,0:T(8,128)(2,1)S(1)} %slice.151), channel_id=1, source_target_pairs={{0,56},{8,0},{16,8},{24,16},{32,24},{40,32},{48,40},{56,48},{1,57}... | collective-permute-start | bytes 589832 | tf_op jit(solution)/shard_map/ppermute | solution.py:181
  38.7 2.5 %collective-permute-done.11.refs_2_ = bf16[6,128,128]{2,1,0:T(8,128)(2,1)S(1)} collective-permute-done((bf16[6,128,128]{2,1,0:T(8,128)(2,1)S(1)}, bf16[6,128,128]{2,1,0:T(8,128)(2,1)S(1)}, u32[]{:S(2)}, u32[]{:S(2)}) %collective-permute-start.11) | collective-permute-done | bytes 196640 | tf_op jit(solution)/shard_map/ppermute | solution.py:181
  41.1 3.5 %collective-permute-done.10.refs_1_ = bf16[6,128,128]{2,1,0:T(8,128)(2,1)S(1)} collective-permute-done((bf16[6,128,128]{2,1,0:T(8,128)(2,1)S(1)}, bf16[6,128,128]{2,1,0:T(8,128)(2,1)S(1)}, u32[]{:S(2)}, u32[]{:S(2)}) %collective-permute-start.10) | collective-permute-done | bytes 196640 | tf_op jit(solution)/shard_map/ppermute | solution.py:181
  44.7 2.6 %shard_map.47 = (bf16[6,128,128]{2,1,0:T(8,128)(2,1)S(1)}, bf16[6,128,128]{2,1,0:T(8,128)(2,1)S(1)}, bf16[6,128,128]{2,1,0:T(8,128)(2,1)S(1)}, bf16[6,128,128]{2,1,0:T(8,128)(2,1)S(1)}) custom-call(s32[24]{0:T(128)S(1)} %pad_add_fusion.6.index_ref, bf16[12,128,128]{2,1,0:T(8,128)(2,1)S(1)} %collective-permute-done.8.refs_0_, ...), custom_call_target="tpu_custom_call" | custom-call | bytes 4194304 | tf_op jit(solution)/shard_map/pallas_call | solution.py:161
  47.4 2.7 %collective-permute-start.13 = (bf16[6,128,128]{2,1,0:T(8,128)(2,1)S(1)}, bf16[6,128,128]{2,1,0:T(8,128)(2,1)S(1)}, u32[]{:S(2)}, u32[]{:S(2)}) collective-permute-start(bf16[6,128,128]{2,1,0:T(8,128)(2,1)S(1)} %get-tuple-element.27), channel_id=1, source_target_pairs={{0,192},{64,0},{128,64},{192,128},{1,193},{65,1},{129,65},{193,129... | collective-permute-start | bytes 589832 | tf_op jit(solution)/shard_map/ppermute | solution.py:181
  51.3 5.8 %collective-permute-start.7 = (bf16[20,128,128]{2,1,0:T(8,128)(2,1)}, bf16[20,128,128]{2,1,0:T(8,128)(2,1)S(1)}, u32[]{:S(2)}, u32[]{:S(2)}) collective-permute-start(bf16[20,128,128]{2,1,0:T(8,128)(2,1)} %pad_maximum_fusion), channel_id=1, source_target_pairs={{0,4},{4,0},{1,5},{5,1},{2,6},{6,2},{3,7},{7,3},{8,12},{12,8},{9,1... | collective-permute-start | bytes 1966088 | tf_op jit(solution)/shard_map/ppermute | solution.py:181
  58.1 5.5 %collective-permute-start.15 = (bf16[12,128,128]{2,1,0:T(8,128)(2,1)}, bf16[12,128,128]{2,1,0:T(8,128)(2,1)S(1)}, u32[]{:S(2)}, u32[]{:S(2)}) collective-permute-start(bf16[12,128,128]{2,1,0:T(8,128)(2,1)} %pad_maximum_fusion.1), channel_id=1, source_target_pairs={{0,4},{4,0},{1,5},{5,1},{2,6},{6,2},{3,7},{7,3},{8,12},{12,8},{9,1... | collective-permute-start | bytes 1179656 | tf_op jit(solution)/shard_map/ppermute | solution.py:181
  65.2 2.9 %shard_map.48 = (bf16[16,128,128]{2,1,0:T(8,128)(2,1)S(1)}, bf16[16,128,128]{2,1,0:T(8,128)(2,1)S(1)}, bf16[16,128,128]{2,1,0:T(8,128)(2,1)S(1)}, bf16[16,128,128]{2,1,0:T(8,128)(2,1)S(1)}) custom-call(s32[64]{0:T(128)S(1)} %pad_add_fusion.4.index_ref, bf16[10,128,128]{2,1,0:T(8,128)(2,1)S(1)} %collective-permute-done.4.refs_0_, ...), custom_call_target="tpu_custom_call" | custom-call | bytes 4194304 | tf_op jit(solution)/shard_map/pallas_call | solution.py:161
  71.0 1.6 collective-permute-start.18
  72.8 9.8 %collective-permute-done.16.refs_0_ = bf16[16,128,128]{2,1,0:T(8,128)(2,1)S(1)} collective-permute-done((bf16[16,128,128]{2,1,0:T(8,128)(2,1)S(1)}, bf16[16,128,128]{2,1,0:T(8,128)(2,1)S(1)}, u32[]{:S(2)}, u32[]{:S(2)}) %collective-permute-start.16) | collective-permute-done | bytes 524320 | tf_op jit(solution)/shard_map/ppermute | solution.py:181
  82.6 12.3 %collective-permute-done.18.refs_2_ = bf16[16,128,128]{2,1,0:T(8,128)(2,1)S(1)} collective-permute-done((bf16[16,128,128]{2,1,0:T(8,128)(2,1)S(1)}, bf16[16,128,128]{2,1,0:T(8,128)(2,1)S(1)}, u32[]{:S(2)}, u32[]{:S(2)}) %collective-permute-start.18) | collective-permute-done | bytes 524320 | tf_op jit(solution)/shard_map/ppermute | solution.py:181
  95.0 14.0 %shard_map.49 = (bf16[16,128,128]{2,1,0:T(8,128)(2,1)S(1)}, bf16[16,128,128]{2,1,0:T(8,128)(2,1)S(1)}, bf16[16,128,128]{2,1,0:T(8,128)(2,1)S(1)}, bf16[16,128,128]{2,1,0:T(8,128)(2,1)S(1)}) custom-call(s32[2,64]{1,0:T(2,128)S(1)} %pad_add_fusion.2.entry_ref, s32[64]{0:T(128)S(1)} %reshape.299.keep_ref, ...), custom_call_target="tpu_custom_call" | custom-call | flops 11000000512 | bytes 5242880 | tf_op jit(solution)/shard_map/pallas_call | solution.py:114
  109.6 2.1 %collective-permute-start.20 = (bf16[16,128,128]{2,1,0:T(8,128)(2,1)S(1)}, bf16[16,128,128]{2,1,0:T(8,128)(2,1)S(1)}, u32[]{:S(2)}, u32[]{:S(2)}) collective-permute-start(bf16[16,128,128]{2,1,0:T(8,128)(2,1)S(1)} %get-tuple-element.35), channel_id=1, source_target_pairs={{0,3},{1,0},{2,1},{3,2},{4,7},{5,4},{6,5},{7,6},{8,11},{9,8},{10,9... | collective-permute-start | bytes 1572872 | tf_op jit(solution)/shard_map/ppermute | solution.py:181
  111.9 11.7 %collective-permute-done.19.refs_0_ = bf16[16,128,128]{2,1,0:T(8,128)(2,1)S(1)} collective-permute-done((bf16[16,128,128]{2,1,0:T(8,128)(2,1)S(1)}, bf16[16,128,128]{2,1,0:T(8,128)(2,1)S(1)}, u32[]{:S(2)}, u32[]{:S(2)}) %collective-permute-start.19) | collective-permute-done | bytes 524320 | tf_op jit(solution)/shard_map/ppermute | solution.py:181
  123.5 9.1 %collective-permute-done.21.refs_2_ = bf16[16,128,128]{2,1,0:T(8,128)(2,1)S(1)} collective-permute-done((bf16[16,128,128]{2,1,0:T(8,128)(2,1)S(1)}, bf16[16,128,128]{2,1,0:T(8,128)(2,1)S(1)}, u32[]{:S(2)}, u32[]{:S(2)}) %collective-permute-start.21) | collective-permute-done | bytes 524320 | tf_op jit(solution)/shard_map/ppermute | solution.py:181
  132.6 2.3 %shard_map.50 = bf16[64,128,128]{2,1,0:T(8,128)(2,1)} custom-call(s32[64]{0:T(128)S(1)} %pad_add_fusion.3.index_ref, bf16[16,128,128]{2,1,0:T(8,128)(2,1)S(1)} %collective-permute-done.19.refs_0_, bf16[16,128,128]{2,1,0:T(8,128)(2,1)S(1)} %collective-permute-done.20.refs_1_, bf16[16,128,128]{2,1,0:T(8,128)(2,1)S(1)} %collective-permute-done.21.refs_2_, ...), custom_call_target="tpu_custom_call" | custom-call | bytes 4194304 | tf_op jit(solution)/shard_map/pallas_call | solution.py:161
  135.0 8.3 %all-to-all-start = ((bf16[64,128,128]{2,1,0:T(8,128)(2,1)}), bf16[64,128,128]{2,1,0:T(8,128)(2,1)S(1)}, u32[]{:S(2)}, u32[]{:S(2)}) async-start(bf16[64,128,128]{2,1,0:T(8,128)(2,1)} %shard_map.50), calls=%async_computation | async-start | bytes 4194304 | tf_op jit(solution)/shard_map/all_to_all | solution.py:277
  143.6 50.9 %all-to-all-done = bf16[64,128,128]{2,1,0:T(8,128)(2,1)S(1)} async-done(((bf16[64,128,128]{2,1,0:T(8,128)(2,1)}), bf16[64,128,128]{2,1,0:T(8,128)(2,1)S(1)}, u32[]{:S(2)}, u32[]{:S(2)}) %all-to-all-start) | async-done | bytes 2097184 | tf_op jit(solution)/shard_map/all_to_all | solution.py:277
  (110 shorter events, 19.3 us)
Async XLA Ops:
  0.0 14.5 %collective-permute-start = (bf16[12,128,128]{2,1,0:T(8,128)(2,1)}, bf16[12,128,128]{2,1,0:T(8,128)(2,1)S(1)}, u32[]{:S(2)}, u32[]{:S(2)}) collective-permute-start(bf16[12,128,128]{2,1,0:T(8,128)(2,1)} %refs_0_.1), channel_id=1, source_target_pairs={{0,56},{8,0},{16,8},{24,16},{32,24},{40,32},{48,40},{56,48},{1,57}... | collective-permute-start | bytes 1179656 | tf_op jit(solution)/shard_map/ppermute | solution.py:181
  6.4 11.4 %collective-permute-start.2 = (bf16[12,128,128]{2,1,0:T(8,128)(2,1)}, bf16[12,128,128]{2,1,0:T(8,128)(2,1)S(1)}, u32[]{:S(2)}, u32[]{:S(2)}) collective-permute-start(bf16[12,128,128]{2,1,0:T(8,128)(2,1)} %refs_0_.1), channel_id=1, source_target_pairs={{0,8},{8,16},{16,24},{24,32},{32,40},{40,48},{48,56},{56,0},{1,9},... | collective-permute-start | bytes 1179656 | tf_op jit(solution)/shard_map/ppermute | solution.py:181
  14.5 10.2 %collective-permute-start.1 = (bf16[12,128,128]{2,1,0:T(8,128)(2,1)S(1)}, bf16[12,128,128]{2,1,0:T(8,128)(2,1)S(1)}, u32[]{:S(2)}, u32[]{:S(2)}) collective-permute-start(bf16[12,128,128]{2,1,0:T(8,128)(2,1)S(1)} %collective-permute-done.refs_1_), channel_id=1, source_target_pairs={{0,56},{8,0},{16,8},{24,16},{32,24},{40,32},{48,40},{56,48},{1,57}... | collective-permute-start | bytes 1179656 | tf_op jit(solution)/shard_map/ppermute | solution.py:181
  17.8 10.3 %collective-permute-start.3 = (bf16[12,128,128]{2,1,0:T(8,128)(2,1)S(1)}, bf16[12,128,128]{2,1,0:T(8,128)(2,1)S(1)}, u32[]{:S(2)}, u32[]{:S(2)}) collective-permute-start(bf16[12,128,128]{2,1,0:T(8,128)(2,1)S(1)} %collective-permute-done.2.refs_4_), channel_id=1, source_target_pairs={{0,8},{8,16},{16,24},{24,32},{32,40},{40,48},{48,56},{56,0},{1,9},... | collective-permute-start | bytes 1179656 | tf_op jit(solution)/shard_map/ppermute | solution.py:181
  24.7 11.1 %collective-permute-start.8 = (bf16[12,128,128]{2,1,0:T(8,128)(2,1)S(1)}, bf16[12,128,128]{2,1,0:T(8,128)(2,1)S(1)}, u32[]{:S(2)}, u32[]{:S(2)}) collective-permute-start(bf16[12,128,128]{2,1,0:T(8,128)(2,1)S(1)} %collective-permute-done.1.refs_2_), channel_id=1, source_target_pairs={{0,56},{8,0},{16,8},{24,16},{32,24},{40,32},{48,40},{56,48},{1,57}... | collective-permute-start | bytes 1179656 | tf_op jit(solution)/shard_map/ppermute | solution.py:181
  28.1 10.4 %collective-permute-start.9 = (bf16[12,128,128]{2,1,0:T(8,128)(2,1)S(1)}, bf16[12,128,128]{2,1,0:T(8,128)(2,1)S(1)}, u32[]{:S(2)}, u32[]{:S(2)}) collective-permute-start(bf16[12,128,128]{2,1,0:T(8,128)(2,1)S(1)} %collective-permute-done.3.refs_3_), channel_id=1, source_target_pairs={{0,8},{8,16},{16,24},{24,32},{32,40},{40,48},{48,56},{56,0},{1,9},... | collective-permute-start | bytes 1179656 | tf_op jit(solution)/shard_map/ppermute | solution.py:181
  31.4 18.7 %collective-permute-start.4 = (bf16[10,128,128]{2,1,0:T(8,128)(2,1)S(1)}, bf16[10,128,128]{2,1,0:T(8,128)(2,1)S(1)}, u32[]{:S(2)}, u32[]{:S(2)}) collective-permute-start(bf16[10,128,128]{2,1,0:T(8,128)(2,1)S(1)} %get-tuple-element.22), channel_id=1, source_target_pairs={{0,64},{64,128},{128,192},{192,0},{1,65},{65,129},{129,193},{193,1... | collective-permute-start | bytes 983048 | tf_op jit(solution)/shard_map/ppermute | solution.py:181
  32.7 17.6 %collective-permute-start.5 = (bf16[10,128,128]{2,1,0:T(8,128)(2,1)S(1)}, bf16[10,128,128]{2,1,0:T(8,128)(2,1)S(1)}, u32[]{:S(2)}, u32[]{:S(2)}) collective-permute-start(bf16[10,128,128]{2,1,0:T(8,128)(2,1)S(1)} %get-tuple-element.23), channel_id=1, source_target_pairs={{0,192},{64,0},{128,64},{192,128},{1,193},{65,1},{129,65},{193,129... | collective-permute-start | bytes 983048 | tf_op jit(solution)/shard_map/ppermute | solution.py:181
  34.2 16.2 %collective-permute-start.6 = (bf16[10,128,128]{2,1,0:T(8,128)(2,1)S(1)}, bf16[10,128,128]{2,1,0:T(8,128)(2,1)S(1)}, u32[]{:S(2)}, u32[]{:S(2)}) collective-permute-start(bf16[10,128,128]{2,1,0:T(8,128)(2,1)S(1)} %get-tuple-element.24), channel_id=1, source_target_pairs={{0,128},{64,192},{128,0},{192,64},{1,129},{65,193},{129,1},{193,65... | collective-permute-start | bytes 983048 | tf_op jit(solution)/shard_map/ppermute | solution.py:181
  35.8 5.4 %collective-permute-start.11 = (bf16[6,128,128]{2,1,0:T(8,128)(2,1)S(1)}, bf16[6,128,128]{2,1,0:T(8,128)(2,1)S(1)}, u32[]{:S(2)}, u32[]{:S(2)}) collective-permute-start(bf16[6,128,128]{2,1,0:T(8,128)(2,1)S(1)} %slice.151), channel_id=1, source_target_pairs={{0,56},{8,0},{16,8},{24,16},{32,24},{40,32},{48,40},{56,48},{1,57}... | collective-permute-start | bytes 589832 | tf_op jit(solution)/shard_map/ppermute | solution.py:181
  38.6 6.1 %collective-permute-start.10 = (bf16[6,128,128]{2,1,0:T(8,128)(2,1)S(1)}, bf16[6,128,128]{2,1,0:T(8,128)(2,1)S(1)}, u32[]{:S(2)}, u32[]{:S(2)}) collective-permute-start(bf16[6,128,128]{2,1,0:T(8,128)(2,1)S(1)} %slice.150), channel_id=1, source_target_pairs={{0,8},{8,16},{16,24},{24,32},{32,40},{40,48},{48,56},{56,0},{1,9},... | collective-permute-start | bytes 589832 | tf_op jit(solution)/shard_map/ppermute | solution.py:181
  47.3 9.9 %collective-permute-start.12 = (bf16[6,128,128]{2,1,0:T(8,128)(2,1)S(1)}, bf16[6,128,128]{2,1,0:T(8,128)(2,1)S(1)}, u32[]{:S(2)}, u32[]{:S(2)}) collective-permute-start(bf16[6,128,128]{2,1,0:T(8,128)(2,1)S(1)} %get-tuple-element.26), channel_id=1, source_target_pairs={{0,64},{64,128},{128,192},{192,0},{1,65},{65,129},{129,193},{193,1... | collective-permute-start | bytes 589832 | tf_op jit(solution)/shard_map/ppermute | solution.py:181
  47.4 9.8 %collective-permute-start.13 = (bf16[6,128,128]{2,1,0:T(8,128)(2,1)S(1)}, bf16[6,128,128]{2,1,0:T(8,128)(2,1)S(1)}, u32[]{:S(2)}, u32[]{:S(2)}) collective-permute-start(bf16[6,128,128]{2,1,0:T(8,128)(2,1)S(1)} %get-tuple-element.27), channel_id=1, source_target_pairs={{0,192},{64,0},{128,64},{192,128},{1,193},{65,1},{129,65},{193,129... | collective-permute-start | bytes 589832 | tf_op jit(solution)/shard_map/ppermute | solution.py:181
  50.1 7.2 %collective-permute-start.14 = (bf16[6,128,128]{2,1,0:T(8,128)(2,1)S(1)}, bf16[6,128,128]{2,1,0:T(8,128)(2,1)S(1)}, u32[]{:S(2)}, u32[]{:S(2)}) collective-permute-start(bf16[6,128,128]{2,1,0:T(8,128)(2,1)S(1)} %get-tuple-element.28), channel_id=1, source_target_pairs={{0,128},{64,192},{128,0},{192,64},{1,129},{65,193},{129,1},{193,65... | collective-permute-start | bytes 589832 | tf_op jit(solution)/shard_map/ppermute | solution.py:181
  51.3 12.7 %collective-permute-start.7 = (bf16[20,128,128]{2,1,0:T(8,128)(2,1)}, bf16[20,128,128]{2,1,0:T(8,128)(2,1)S(1)}, u32[]{:S(2)}, u32[]{:S(2)}) collective-permute-start(bf16[20,128,128]{2,1,0:T(8,128)(2,1)} %pad_maximum_fusion), channel_id=1, source_target_pairs={{0,4},{4,0},{1,5},{5,1},{2,6},{6,2},{3,7},{7,3},{8,12},{12,8},{9,1... | collective-permute-start | bytes 1966088 | tf_op jit(solution)/shard_map/ppermute | solution.py:181
  57.2 37.7 %copy-start.1 = (bf16[1024,128]{1,0:T(8,128)(2,1)S(1)}, bf16[1024,128]{1,0:T(8,128)(2,1)}, u32[]{:S(2)}) copy-start(bf16[1024,128]{1,0:T(8,128)(2,1)} %refs_4_.1) | copy-start | bytes 786436
  58.1 7.1 %collective-permute-start.15 = (bf16[12,128,128]{2,1,0:T(8,128)(2,1)}, bf16[12,128,128]{2,1,0:T(8,128)(2,1)S(1)}, u32[]{:S(2)}, u32[]{:S(2)}) collective-permute-start(bf16[12,128,128]{2,1,0:T(8,128)(2,1)} %pad_maximum_fusion.1), channel_id=1, source_target_pairs={{0,4},{4,0},{1,5},{5,1},{2,6},{6,2},{3,7},{7,3},{8,12},{12,8},{9,1... | collective-permute-start | bytes 1179656 | tf_op jit(solution)/shard_map/ppermute | solution.py:181
  68.1 14.6 %collective-permute-start.16 = (bf16[16,128,128]{2,1,0:T(8,128)(2,1)S(1)}, bf16[16,128,128]{2,1,0:T(8,128)(2,1)S(1)}, u32[]{:S(2)}, u32[]{:S(2)}) collective-permute-start(bf16[16,128,128]{2,1,0:T(8,128)(2,1)S(1)} %get-tuple-element.30), channel_id=1, source_target_pairs={{0,1},{1,2},{2,3},{3,0},{4,5},{5,6},{6,7},{7,4},{8,9},{9,10},{10,1... | collective-permute-start | bytes 1572872 | tf_op jit(solution)/shard_map/ppermute | solution.py:181
  69.4 13.2 %collective-permute-start.17 = (bf16[16,128,128]{2,1,0:T(8,128)(2,1)S(1)}, bf16[16,128,128]{2,1,0:T(8,128)(2,1)S(1)}, u32[]{:S(2)}, u32[]{:S(2)}) collective-permute-start(bf16[16,128,128]{2,1,0:T(8,128)(2,1)S(1)} %get-tuple-element.31), channel_id=1, source_target_pairs={{0,3},{1,0},{2,1},{3,2},{4,7},{5,4},{6,5},{7,6},{8,11},{9,8},{10,9... | collective-permute-start | bytes 1572872 | tf_op jit(solution)/shard_map/ppermute | solution.py:181
  71.0 24.0 %collective-permute-start.18 = (bf16[16,128,128]{2,1,0:T(8,128)(2,1)S(1)}, bf16[16,128,128]{2,1,0:T(8,128)(2,1)S(1)}, u32[]{:S(2)}, u32[]{:S(2)}) collective-permute-start(bf16[16,128,128]{2,1,0:T(8,128)(2,1)S(1)} %get-tuple-element.32), channel_id=1, source_target_pairs={{0,2},{1,3},{2,0},{3,1},{4,6},{5,7},{6,4},{7,5},{8,10},{9,11},{10,... | collective-permute-start | bytes 1572872 | tf_op jit(solution)/shard_map/ppermute | solution.py:181
  109.0 14.6 %collective-permute-start.19 = (bf16[16,128,128]{2,1,0:T(8,128)(2,1)S(1)}, bf16[16,128,128]{2,1,0:T(8,128)(2,1)S(1)}, u32[]{:S(2)}, u32[]{:S(2)}) collective-permute-start(bf16[16,128,128]{2,1,0:T(8,128)(2,1)S(1)} %get-tuple-element.34), channel_id=1, source_target_pairs={{0,1},{1,2},{2,3},{3,0},{4,5},{5,6},{6,7},{7,4},{8,9},{9,10},{10,1... | collective-permute-start | bytes 1572872 | tf_op jit(solution)/shard_map/ppermute | solution.py:181
  109.6 13.9 %collective-permute-start.20 = (bf16[16,128,128]{2,1,0:T(8,128)(2,1)S(1)}, bf16[16,128,128]{2,1,0:T(8,128)(2,1)S(1)}, u32[]{:S(2)}, u32[]{:S(2)}) collective-permute-start(bf16[16,128,128]{2,1,0:T(8,128)(2,1)S(1)} %get-tuple-element.35), channel_id=1, source_target_pairs={{0,3},{1,0},{2,1},{3,2},{4,7},{5,4},{6,5},{7,6},{8,11},{9,8},{10,9... | collective-permute-start | bytes 1572872 | tf_op jit(solution)/shard_map/ppermute | solution.py:181
  111.7 20.9 %collective-permute-start.21 = (bf16[16,128,128]{2,1,0:T(8,128)(2,1)S(1)}, bf16[16,128,128]{2,1,0:T(8,128)(2,1)S(1)}, u32[]{:S(2)}, u32[]{:S(2)}) collective-permute-start(bf16[16,128,128]{2,1,0:T(8,128)(2,1)S(1)} %get-tuple-element.36), channel_id=1, source_target_pairs={{0,2},{1,3},{2,0},{3,1},{4,6},{5,7},{6,4},{7,5},{8,10},{9,11},{10,... | collective-permute-start | bytes 1572872 | tf_op jit(solution)/shard_map/ppermute | solution.py:181
  135.0 59.5 %all-to-all-start = ((bf16[64,128,128]{2,1,0:T(8,128)(2,1)}), bf16[64,128,128]{2,1,0:T(8,128)(2,1)S(1)}, u32[]{:S(2)}, u32[]{:S(2)}) async-start(bf16[64,128,128]{2,1,0:T(8,128)(2,1)} %shard_map.50), calls=%async_computation | async-start | bytes 4194304 | tf_op jit(solution)/shard_map/all_to_all | solution.py:277
  (3 other events, 22.6 us)

commit v4 on v3

--- a/solution.py
+++ b/solution.py
@@ -49,7 +49,7 @@
     for copy, ref, start in zip(arrivals, blocks, starts_of(blocks)):
         copy.wait()
 
-        @pl.loop(start, start + ref.shape[0], unroll=4)
+        @pl.loop(start, start + ref.shape[0], unroll=16)
         def place(j):
             entry = entry_ref[0, j]
             x[at(entry // edge, width), at(entry % edge, width)] = kept(staged[j], entry)
@@ -93,7 +93,7 @@
     departures = bulk(outs, staged, sent, False)
     for copy, ref, start in zip(departures, outs, starts_of(outs)):
 
-        @pl.loop(start, start + ref.shape[0], unroll=4)
+        @pl.loop(start, start + ref.shape[0], unroll=16)
         def send(j):
             entry = entry_ref[1, j]
             block = grad_t[at(entry % edge, width), at(entry // edge, width)]
@@ -139,7 +139,7 @@
             for copy, ref, start in zip(arrivals, ins, starts_of(ins)):
                 copy.wait()
 
-                @pl.loop(start, start + ref.shape[0], unroll=4)
+                @pl.loop(start, start + ref.shape[0], unroll=16)
                 def _(j):
                     leaves[index_ref[j]] = came[j]
 

time: 197 us -> 197 us (level)
  no operation moved by 1% of the time
where the time goes in v4:
time: 197 us; the launch traced here: 196 us
  waiting for transfers between devices  112 us (57%)
  starting transfers between devices  50.2 us (25%)
  Pallas kernels  23.4 us (12%)
  local copies, waits for them, and re-layouts  4.81 us (2%)
  other arithmetic  3.82 us (2%)
    ppermute x22, waiting for transfers between devices, shift(): lax.ppermute(blocks, axis, [(i, (i + step) % count) for i in range(count)])  61.6 us
    all_to_all x1, waiting for transfers between devices, shards(): lax.all_to_all(held, AXES[:3], split_axis=0, concat_axis=0, tiled=True)  50.9 us
    ppermute x22, starting transfers between devices, shift(): lax.ppermute(blocks, axis, [(i, (i + step) % count) for i in range(count)])  41.8 us
    pallas_call x1, Pallas kernels, adjoint_pieces(): pl.pallas_call(functools.partial(adjoint_kernel, span, arrays), out_shape...  13.5 us
    pallas_call x4, Pallas kernels, arrange(): pl.pallas_call(kernel, out_shape=[jax.ShapeDtypeStruct((count, *shape), d...  9.93 us
    all_to_all x1, starting transfers between devices, shards(): lax.all_to_all(held, AXES[:3], split_axis=0, concat_axis=0, tiled=True)  8.36 us
  transfers between devices with their start and end apart: 23, of which 10 were waited for; matrix products, arithmetic and copies ran while one was open for 3% of the time, Pallas kernels for 2%

profile of v4, /device:TPU:1, one launch (start us, length us, event | category | flops | bytes accessed | tf_op | source)
XLA Modules:
  0.0 196.4 jit_solution(13818231453700732930)
XLA Ops:
  0.0 6.4 %collective-permute-start = (bf16[12,128,128]{2,1,0:T(8,128)(2,1)}, bf16[12,128,128]{2,1,0:T(8,128)(2,1)S(1)}, u32[]{:S(2)}, u32[]{:S(2)}) collective-permute-start(bf16[12,128,128]{2,1,0:T(8,128)(2,1)} %refs_0_.1), channel_id=1, source_target_pairs={{0,56},{8,0},{16,8},{24,16},{32,24},{40,32},{48,40},{56,48},{1,57}... | collective-permute-start | bytes 1179656 | tf_op jit(solution)/shard_map/ppermute | solution.py:181
  8.6 5.9 %collective-permute-done.refs_1_ = bf16[12,128,128]{2,1,0:T(8,128)(2,1)S(1)} collective-permute-done((bf16[12,128,128]{2,1,0:T(8,128)(2,1)}, bf16[12,128,128]{2,1,0:T(8,128)(2,1)S(1)}, u32[]{:S(2)}, u32[]{:S(2)}) %collective-permute-start) | collective-permute-done | bytes 393248 | tf_op jit(solution)/shard_map/ppermute | solution.py:181
  14.5 3.3 %collective-permute-start.1 = (bf16[12,128,128]{2,1,0:T(8,128)(2,1)S(1)}, bf16[12,128,128]{2,1,0:T(8,128)(2,1)S(1)}, u32[]{:S(2)}, u32[]{:S(2)}) collective-permute-start(bf16[12,128,128]{2,1,0:T(8,128)(2,1)S(1)} %collective-permute-done.refs_1_), channel_id=1, source_target_pairs={{0,56},{8,0},{16,8},{24,16},{32,24},{40,32},{48,40},{56,48},{1,57}... | collective-permute-start | bytes 1179656 | tf_op jit(solution)/shard_map/ppermute | solution.py:181
  19.1 5.6 %collective-permute-done.1.refs_2_ = bf16[12,128,128]{2,1,0:T(8,128)(2,1)S(1)} collective-permute-done((bf16[12,128,128]{2,1,0:T(8,128)(2,1)S(1)}, bf16[12,128,128]{2,1,0:T(8,128)(2,1)S(1)}, u32[]{:S(2)}, u32[]{:S(2)}) %collective-permute-start.1) | collective-permute-done | bytes 393248 | tf_op jit(solution)/shard_map/ppermute | solution.py:181
  24.7 3.4 %collective-permute-start.8 = (bf16[12,128,128]{2,1,0:T(8,128)(2,1)S(1)}, bf16[12,128,128]{2,1,0:T(8,128)(2,1)S(1)}, u32[]{:S(2)}, u32[]{:S(2)}) collective-permute-start(bf16[12,128,128]{2,1,0:T(8,128)(2,1)S(1)} %collective-permute-done.1.refs_2_), channel_id=1, source_target_pairs={{0,56},{8,0},{16,8},{24,16},{32,24},{40,32},{48,40},{56,48},{1,57}... | collective-permute-start | bytes 1179656 | tf_op jit(solution)/shard_map/ppermute | solution.py:181
  29.2 2.2 %shard_map.46 = (bf16[10,128,128]{2,1,0:T(8,128)(2,1)S(1)}, bf16[10,128,128]{2,1,0:T(8,128)(2,1)S(1)}, bf16[10,128,128]{2,1,0:T(8,128)(2,1)S(1)}, bf16[10,128,128]{2,1,0:T(8,128)(2,1)S(1)}) custom-call(s32[40]{0:T(128)S(1)} %pad_add_fusion.5.index_ref, bf16[12,128,128]{2,1,0:T(8,128)(2,1)S(1)} %copy-done, ...), custom_call_target="tpu_custom_call" | custom-call | bytes 4194304 | tf_op jit(solution)/shard_map/pallas_call | solution.py:161
  35.8 2.7 %collective-permute-start.11 = (bf16[6,128,128]{2,1,0:T(8,128)(2,1)S(1)}, bf16[6,128,128]{2,1,0:T(8,128)(2,1)S(1)}, u32[]{:S(2)}, u32[]{:S(2)}) collective-permute-start(bf16[6,128,128]{2,1,0:T(8,128)(2,1)S(1)} %slice.151), channel_id=1, source_target_pairs={{0,56},{8,0},{16,8},{24,16},{32,24},{40,32},{48,40},{56,48},{1,57}... | collective-permute-start | bytes 589832 | tf_op jit(solution)/shard_map/ppermute | solution.py:181
  38.7 2.5 %collective-permute-done.11.refs_2_ = bf16[6,128,128]{2,1,0:T(8,128)(2,1)S(1)} collective-permute-done((bf16[6,128,128]{2,1,0:T(8,128)(2,1)S(1)}, bf16[6,128,128]{2,1,0:T(8,128)(2,1)S(1)}, u32[]{:S(2)}, u32[]{:S(2)}) %collective-permute-start.11) | collective-permute-done | bytes 196640 | tf_op jit(solution)/shard_map/ppermute | solution.py:181
  41.1 3.5 %collective-permute-done.10.refs_1_ = bf16[6,128,128]{2,1,0:T(8,128)(2,1)S(1)} collective-permute-done((bf16[6,128,128]{2,1,0:T(8,128)(2,1)S(1)}, bf16[6,128,128]{2,1,0:T(8,128)(2,1)S(1)}, u32[]{:S(2)}, u32[]{:S(2)}) %collective-permute-start.10) | collective-permute-done | bytes 196640 | tf_op jit(solution)/shard_map/ppermute | solution.py:181
  44.7 2.6 %shard_map.47 = (bf16[6,128,128]{2,1,0:T(8,128)(2,1)S(1)}, bf16[6,128,128]{2,1,0:T(8,128)(2,1)S(1)}, bf16[6,128,128]{2,1,0:T(8,128)(2,1)S(1)}, bf16[6,128,128]{2,1,0:T(8,128)(2,1)S(1)}) custom-call(s32[24]{0:T(128)S(1)} %pad_add_fusion.6.index_ref, bf16[12,128,128]{2,1,0:T(8,128)(2,1)S(1)} %collective-permute-done.8.refs_0_, ...), custom_call_target="tpu_custom_call" | custom-call | bytes 4194304 | tf_op jit(solution)/shard_map/pallas_call | solution.py:161
  47.4 2.7 %collective-permute-start.13 = (bf16[6,128,128]{2,1,0:T(8,128)(2,1)S(1)}, bf16[6,128,128]{2,1,0:T(8,128)(2,1)S(1)}, u32[]{:S(2)}, u32[]{:S(2)}) collective-permute-start(bf16[6,128,128]{2,1,0:T(8,128)(2,1)S(1)} %get-tuple-element.27), channel_id=1, source_target_pairs={{0,192},{64,0},{128,64},{192,128},{1,193},{65,1},{129,65},{193,129... | collective-permute-start | bytes 589832 | tf_op jit(solution)/shard_map/ppermute | solution.py:181
  51.3 5.8 %collective-permute-start.7 = (bf16[20,128,128]{2,1,0:T(8,128)(2,1)}, bf16[20,128,128]{2,1,0:T(8,128)(2,1)S(1)}, u32[]{:S(2)}, u32[]{:S(2)}) collective-permute-start(bf16[20,128,128]{2,1,0:T(8,128)(2,1)} %pad_maximum_fusion), channel_id=1, source_target_pairs={{0,4},{4,0},{1,5},{5,1},{2,6},{6,2},{3,7},{7,3},{8,12},{12,8},{9,1... | collective-permute-start | bytes 1966088 | tf_op jit(solution)/shard_map/ppermute | solution.py:181
  58.1 5.5 %collective-permute-start.15 = (bf16[12,128,128]{2,1,0:T(8,128)(2,1)}, bf16[12,128,128]{2,1,0:T(8,128)(2,1)S(1)}, u32[]{:S(2)}, u32[]{:S(2)}) collective-permute-start(bf16[12,128,128]{2,1,0:T(8,128)(2,1)} %pad_maximum_fusion.1), channel_id=1, source_target_pairs={{0,4},{4,0},{1,5},{5,1},{2,6},{6,2},{3,7},{7,3},{8,12},{12,8},{9,1... | collective-permute-start | bytes 1179656 | tf_op jit(solution)/shard_map/ppermute | solution.py:181
  65.2 2.9 %shard_map.48 = (bf16[16,128,128]{2,1,0:T(8,128)(2,1)S(1)}, bf16[16,128,128]{2,1,0:T(8,128)(2,1)S(1)}, bf16[16,128,128]{2,1,0:T(8,128)(2,1)S(1)}, bf16[16,128,128]{2,1,0:T(8,128)(2,1)S(1)}) custom-call(s32[64]{0:T(128)S(1)} %pad_add_fusion.4.index_ref, bf16[10,128,128]{2,1,0:T(8,128)(2,1)S(1)} %collective-permute-done.4.refs_0_, ...), custom_call_target="tpu_custom_call" | custom-call | bytes 4194304 | tf_op jit(solution)/shard_map/pallas_call | solution.py:161
  71.0 1.6 collective-permute-start.18
  72.8 9.8 %collective-permute-done.16.refs_0_ = bf16[16,128,128]{2,1,0:T(8,128)(2,1)S(1)} collective-permute-done((bf16[16,128,128]{2,1,0:T(8,128)(2,1)S(1)}, bf16[16,128,128]{2,1,0:T(8,128)(2,1)S(1)}, u32[]{:S(2)}, u32[]{:S(2)}) %collective-permute-start.16) | collective-permute-done | bytes 524320 | tf_op jit(solution)/shard_map/ppermute | solution.py:181
  82.6 12.3 %collective-permute-done.18.refs_2_ = bf16[16,128,128]{2,1,0:T(8,128)(2,1)S(1)} collective-permute-done((bf16[16,128,128]{2,1,0:T(8,128)(2,1)S(1)}, bf16[16,128,128]{2,1,0:T(8,128)(2,1)S(1)}, u32[]{:S(2)}, u32[]{:S(2)}) %collective-permute-start.18) | collective-permute-done | bytes 524320 | tf_op jit(solution)/shard_map/ppermute | solution.py:181
  95.0 13.5 %shard_map.49 = (bf16[16,128,128]{2,1,0:T(8,128)(2,1)S(1)}, bf16[16,128,128]{2,1,0:T(8,128)(2,1)S(1)}, bf16[16,128,128]{2,1,0:T(8,128)(2,1)S(1)}, bf16[16,128,128]{2,1,0:T(8,128)(2,1)S(1)}) custom-call(s32[2,64]{1,0:T(2,128)S(1)} %pad_add_fusion.2.entry_ref, s32[64]{0:T(128)S(1)} %reshape.299.keep_ref, ...), custom_call_target="tpu_custom_call" | custom-call | flops 11000000512 | bytes 5242880 | tf_op jit(solution)/shard_map/pallas_call | solution.py:114
  109.1 2.1 %collective-permute-start.20 = (bf16[16,128,128]{2,1,0:T(8,128)(2,1)S(1)}, bf16[16,128,128]{2,1,0:T(8,128)(2,1)S(1)}, u32[]{:S(2)}, u32[]{:S(2)}) collective-permute-start(bf16[16,128,128]{2,1,0:T(8,128)(2,1)S(1)} %get-tuple-element.35), channel_id=1, source_target_pairs={{0,3},{1,0},{2,1},{3,2},{4,7},{5,4},{6,5},{7,6},{8,11},{9,8},{10,9... | collective-permute-start | bytes 1572872 | tf_op jit(solution)/shard_map/ppermute | solution.py:181
  111.4 11.8 %collective-permute-done.19.refs_0_ = bf16[16,128,128]{2,1,0:T(8,128)(2,1)S(1)} collective-permute-done((bf16[16,128,128]{2,1,0:T(8,128)(2,1)S(1)}, bf16[16,128,128]{2,1,0:T(8,128)(2,1)S(1)}, u32[]{:S(2)}, u32[]{:S(2)}) %collective-permute-start.19) | collective-permute-done | bytes 524320 | tf_op jit(solution)/shard_map/ppermute | solution.py:181
  123.2 8.9 %collective-permute-done.21.refs_2_ = bf16[16,128,128]{2,1,0:T(8,128)(2,1)S(1)} collective-permute-done((bf16[16,128,128]{2,1,0:T(8,128)(2,1)S(1)}, bf16[16,128,128]{2,1,0:T(8,128)(2,1)S(1)}, u32[]{:S(2)}, u32[]{:S(2)}) %collective-permute-start.21) | collective-permute-done | bytes 524320 | tf_op jit(solution)/shard_map/ppermute | solution.py:181
  132.1 2.2 %shard_map.50 = bf16[64,128,128]{2,1,0:T(8,128)(2,1)} custom-call(s32[64]{0:T(128)S(1)} %pad_add_fusion.3.index_ref, bf16[16,128,128]{2,1,0:T(8,128)(2,1)S(1)} %collective-permute-done.19.refs_0_, bf16[16,128,128]{2,1,0:T(8,128)(2,1)S(1)} %collective-permute-done.20.refs_1_, bf16[16,128,128]{2,1,0:T(8,128)(2,1)S(1)} %collective-permute-done.21.refs_2_, ...), custom_call_target="tpu_custom_call" | custom-call | bytes 4194304 | tf_op jit(solution)/shard_map/pallas_call | solution.py:161
  134.3 8.4 %all-to-all-start = ((bf16[64,128,128]{2,1,0:T(8,128)(2,1)}), bf16[64,128,128]{2,1,0:T(8,128)(2,1)S(1)}, u32[]{:S(2)}, u32[]{:S(2)}) async-start(bf16[64,128,128]{2,1,0:T(8,128)(2,1)} %shard_map.50), calls=%async_computation | async-start | bytes 4194304 | tf_op jit(solution)/shard_map/all_to_all | solution.py:277
  143.0 50.9 %all-to-all-done = bf16[64,128,128]{2,1,0:T(8,128)(2,1)S(1)} async-done(((bf16[64,128,128]{2,1,0:T(8,128)(2,1)}), bf16[64,128,128]{2,1,0:T(8,128)(2,1)S(1)}, u32[]{:S(2)}, u32[]{:S(2)}) %all-to-all-start) | async-done | bytes 2097184 | tf_op jit(solution)/shard_map/all_to_all | solution.py:277
  (110 shorter events, 19.3 us)
Async XLA Ops:
  0.0 14.5 %collective-permute-start = (bf16[12,128,128]{2,1,0:T(8,128)(2,1)}, bf16[12,128,128]{2,1,0:T(8,128)(2,1)S(1)}, u32[]{:S(2)}, u32[]{:S(2)}) collective-permute-start(bf16[12,128,128]{2,1,0:T(8,128)(2,1)} %refs_0_.1), channel_id=1, source_target_pairs={{0,56},{8,0},{16,8},{24,16},{32,24},{40,32},{48,40},{56,48},{1,57}... | collective-permute-start | bytes 1179656 | tf_op jit(solution)/shard_map/ppermute | solution.py:181
  6.4 11.4 %collective-permute-start.2 = (bf16[12,128,128]{2,1,0:T(8,128)(2,1)}, bf16[12,128,128]{2,1,0:T(8,128)(2,1)S(1)}, u32[]{:S(2)}, u32[]{:S(2)}) collective-permute-start(bf16[12,128,128]{2,1,0:T(8,128)(2,1)} %refs_0_.1), channel_id=1, source_target_pairs={{0,8},{8,16},{16,24},{24,32},{32,40},{40,48},{48,56},{56,0},{1,9},... | collective-permute-start | bytes 1179656 | tf_op jit(solution)/shard_map/ppermute | solution.py:181
  14.5 10.2 %collective-permute-start.1 = (bf16[12,128,128]{2,1,0:T(8,128)(2,1)S(1)}, bf16[12,128,128]{2,1,0:T(8,128)(2,1)S(1)}, u32[]{:S(2)}, u32[]{:S(2)}) collective-permute-start(bf16[12,128,128]{2,1,0:T(8,128)(2,1)S(1)} %collective-permute-done.refs_1_), channel_id=1, source_target_pairs={{0,56},{8,0},{16,8},{24,16},{32,24},{40,32},{48,40},{56,48},{1,57}... | collective-permute-start | bytes 1179656 | tf_op jit(solution)/shard_map/ppermute | solution.py:181
  17.8 10.3 %collective-permute-start.3 = (bf16[12,128,128]{2,1,0:T(8,128)(2,1)S(1)}, bf16[12,128,128]{2,1,0:T(8,128)(2,1)S(1)}, u32[]{:S(2)}, u32[]{:S(2)}) collective-permute-start(bf16[12,128,128]{2,1,0:T(8,128)(2,1)S(1)} %collective-permute-done.2.refs_4_), channel_id=1, source_target_pairs={{0,8},{8,16},{16,24},{24,32},{32,40},{40,48},{48,56},{56,0},{1,9},... | collective-permute-start | bytes 1179656 | tf_op jit(solution)/shard_map/ppermute | solution.py:181
  24.7 11.1 %collective-permute-start.8 = (bf16[12,128,128]{2,1,0:T(8,128)(2,1)S(1)}, bf16[12,128,128]{2,1,0:T(8,128)(2,1)S(1)}, u32[]{:S(2)}, u32[]{:S(2)}) collective-permute-start(bf16[12,128,128]{2,1,0:T(8,128)(2,1)S(1)} %collective-permute-done.1.refs_2_), channel_id=1, source_target_pairs={{0,56},{8,0},{16,8},{24,16},{32,24},{40,32},{48,40},{56,48},{1,57}... | collective-permute-start | bytes 1179656 | tf_op jit(solution)/shard_map/ppermute | solution.py:181
  28.1 10.4 %collective-permute-start.9 = (bf16[12,128,128]{2,1,0:T(8,128)(2,1)S(1)}, bf16[12,128,128]{2,1,0:T(8,128)(2,1)S(1)}, u32[]{:S(2)}, u32[]{:S(2)}) collective-permute-start(bf16[12,128,128]{2,1,0:T(8,128)(2,1)S(1)} %collective-permute-done.3.refs_3_), channel_id=1, source_target_pairs={{0,8},{8,16},{16,24},{24,32},{32,40},{40,48},{48,56},{56,0},{1,9},... | collective-permute-start | bytes 1179656 | tf_op jit(solution)/shard_map/ppermute | solution.py:181
  31.4 18.7 %collective-permute-start.4 = (bf16[10,128,128]{2,1,0:T(8,128)(2,1)S(1)}, bf16[10,128,128]{2,1,0:T(8,128)(2,1)S(1)}, u32[]{:S(2)}, u32[]{:S(2)}) collective-permute-start(bf16[10,128,128]{2,1,0:T(8,128)(2,1)S(1)} %get-tuple-element.22), channel_id=1, source_target_pairs={{0,64},{64,128},{128,192},{192,0},{1,65},{65,129},{129,193},{193,1... | collective-permute-start | bytes 983048 | tf_op jit(solution)/shard_map/ppermute | solution.py:181
  32.7 17.6 %collective-permute-start.5 = (bf16[10,128,128]{2,1,0:T(8,128)(2,1)S(1)}, bf16[10,128,128]{2,1,0:T(8,128)(2,1)S(1)}, u32[]{:S(2)}, u32[]{:S(2)}) collective-permute-start(bf16[10,128,128]{2,1,0:T(8,128)(2,1)S(1)} %get-tuple-element.23), channel_id=1, source_target_pairs={{0,192},{64,0},{128,64},{192,128},{1,193},{65,1},{129,65},{193,129... | collective-permute-start | bytes 983048 | tf_op jit(solution)/shard_map/ppermute | solution.py:181
  34.2 16.2 %collective-permute-start.6 = (bf16[10,128,128]{2,1,0:T(8,128)(2,1)S(1)}, bf16[10,128,128]{2,1,0:T(8,128)(2,1)S(1)}, u32[]{:S(2)}, u32[]{:S(2)}) collective-permute-start(bf16[10,128,128]{2,1,0:T(8,128)(2,1)S(1)} %get-tuple-element.24), channel_id=1, source_target_pairs={{0,128},{64,192},{128,0},{192,64},{1,129},{65,193},{129,1},{193,65... | collective-permute-start | bytes 983048 | tf_op jit(solution)/shard_map/ppermute | solution.py:181
  35.8 5.4 %collective-permute-start.11 = (bf16[6,128,128]{2,1,0:T(8,128)(2,1)S(1)}, bf16[6,128,128]{2,1,0:T(8,128)(2,1)S(1)}, u32[]{:S(2)}, u32[]{:S(2)}) collective-permute-start(bf16[6,128,128]{2,1,0:T(8,128)(2,1)S(1)} %slice.151), channel_id=1, source_target_pairs={{0,56},{8,0},{16,8},{24,16},{32,24},{40,32},{48,40},{56,48},{1,57}... | collective-permute-start | bytes 589832 | tf_op jit(solution)/shard_map/ppermute | solution.py:181
  38.6 6.1 %collective-permute-start.10 = (bf16[6,128,128]{2,1,0:T(8,128)(2,1)S(1)}, bf16[6,128,128]{2,1,0:T(8,128)(2,1)S(1)}, u32[]{:S(2)}, u32[]{:S(2)}) collective-permute-start(bf16[6,128,128]{2,1,0:T(8,128)(2,1)S(1)} %slice.150), channel_id=1, source_target_pairs={{0,8},{8,16},{16,24},{24,32},{32,40},{40,48},{48,56},{56,0},{1,9},... | collective-permute-start | bytes 589832 | tf_op jit(solution)/shard_map/ppermute | solution.py:181
  47.3 9.9 %collective-permute-start.12 = (bf16[6,128,128]{2,1,0:T(8,128)(2,1)S(1)}, bf16[6,128,128]{2,1,0:T(8,128)(2,1)S(1)}, u32[]{:S(2)}, u32[]{:S(2)}) collective-permute-start(bf16[6,128,128]{2,1,0:T(8,128)(2,1)S(1)} %get-tuple-element.26), channel_id=1, source_target_pairs={{0,64},{64,128},{128,192},{192,0},{1,65},{65,129},{129,193},{193,1... | collective-permute-start | bytes 589832 | tf_op jit(solution)/shard_map/ppermute | solution.py:181
  47.4 9.8 %collective-permute-start.13 = (bf16[6,128,128]{2,1,0:T(8,128)(2,1)S(1)}, bf16[6,128,128]{2,1,0:T(8,128)(2,1)S(1)}, u32[]{:S(2)}, u32[]{:S(2)}) collective-permute-start(bf16[6,128,128]{2,1,0:T(8,128)(2,1)S(1)} %get-tuple-element.27), channel_id=1, source_target_pairs={{0,192},{64,0},{128,64},{192,128},{1,193},{65,1},{129,65},{193,129... | collective-permute-start | bytes 589832 | tf_op jit(solution)/shard_map/ppermute | solution.py:181
  50.1 7.2 %collective-permute-start.14 = (bf16[6,128,128]{2,1,0:T(8,128)(2,1)S(1)}, bf16[6,128,128]{2,1,0:T(8,128)(2,1)S(1)}, u32[]{:S(2)}, u32[]{:S(2)}) collective-permute-start(bf16[6,128,128]{2,1,0:T(8,128)(2,1)S(1)} %get-tuple-element.28), channel_id=1, source_target_pairs={{0,128},{64,192},{128,0},{192,64},{1,129},{65,193},{129,1},{193,65... | collective-permute-start | bytes 589832 | tf_op jit(solution)/shard_map/ppermute | solution.py:181
  51.3 12.7 %collective-permute-start.7 = (bf16[20,128,128]{2,1,0:T(8,128)(2,1)}, bf16[20,128,128]{2,1,0:T(8,128)(2,1)S(1)}, u32[]{:S(2)}, u32[]{:S(2)}) collective-permute-start(bf16[20,128,128]{2,1,0:T(8,128)(2,1)} %pad_maximum_fusion), channel_id=1, source_target_pairs={{0,4},{4,0},{1,5},{5,1},{2,6},{6,2},{3,7},{7,3},{8,12},{12,8},{9,1... | collective-permute-start | bytes 1966088 | tf_op jit(solution)/shard_map/ppermute | solution.py:181
  57.2 37.7 %copy-start.1 = (bf16[1024,128]{1,0:T(8,128)(2,1)S(1)}, bf16[1024,128]{1,0:T(8,128)(2,1)}, u32[]{:S(2)}) copy-start(bf16[1024,128]{1,0:T(8,128)(2,1)} %refs_4_.1) | copy-start | bytes 786436
  58.1 7.1 %collective-permute-start.15 = (bf16[12,128,128]{2,1,0:T(8,128)(2,1)}, bf16[12,128,128]{2,1,0:T(8,128)(2,1)S(1)}, u32[]{:S(2)}, u32[]{:S(2)}) collective-permute-start(bf16[12,128,128]{2,1,0:T(8,128)(2,1)} %pad_maximum_fusion.1), channel_id=1, source_target_pairs={{0,4},{4,0},{1,5},{5,1},{2,6},{6,2},{3,7},{7,3},{8,12},{12,8},{9,1... | collective-permute-start | bytes 1179656 | tf_op jit(solution)/shard_map/ppermute | solution.py:181
  68.1 14.6 %collective-permute-start.16 = (bf16[16,128,128]{2,1,0:T(8,128)(2,1)S(1)}, bf16[16,128,128]{2,1,0:T(8,128)(2,1)S(1)}, u32[]{:S(2)}, u32[]{:S(2)}) collective-permute-start(bf16[16,128,128]{2,1,0:T(8,128)(2,1)S(1)} %get-tuple-element.30), channel_id=1, source_target_pairs={{0,1},{1,2},{2,3},{3,0},{4,5},{5,6},{6,7},{7,4},{8,9},{9,10},{10,1... | collective-permute-start | bytes 1572872 | tf_op jit(solution)/shard_map/ppermute | solution.py:181
  69.4 13.2 %collective-permute-start.17 = (bf16[16,128,128]{2,1,0:T(8,128)(2,1)S(1)}, bf16[16,128,128]{2,1,0:T(8,128)(2,1)S(1)}, u32[]{:S(2)}, u32[]{:S(2)}) collective-permute-start(bf16[16,128,128]{2,1,0:T(8,128)(2,1)S(1)} %get-tuple-element.31), channel_id=1, source_target_pairs={{0,3},{1,0},{2,1},{3,2},{4,7},{5,4},{6,5},{7,6},{8,11},{9,8},{10,9... | collective-permute-start | bytes 1572872 | tf_op jit(solution)/shard_map/ppermute | solution.py:181
  71.0 24.0 %collective-permute-start.18 = (bf16[16,128,128]{2,1,0:T(8,128)(2,1)S(1)}, bf16[16,128,128]{2,1,0:T(8,128)(2,1)S(1)}, u32[]{:S(2)}, u32[]{:S(2)}) collective-permute-start(bf16[16,128,128]{2,1,0:T(8,128)(2,1)S(1)} %get-tuple-element.32), channel_id=1, source_target_pairs={{0,2},{1,3},{2,0},{3,1},{4,6},{5,7},{6,4},{7,5},{8,10},{9,11},{10,... | collective-permute-start | bytes 1572872 | tf_op jit(solution)/shard_map/ppermute | solution.py:181
  108.5 14.7 %collective-permute-start.19 = (bf16[16,128,128]{2,1,0:T(8,128)(2,1)S(1)}, bf16[16,128,128]{2,1,0:T(8,128)(2,1)S(1)}, u32[]{:S(2)}, u32[]{:S(2)}) collective-permute-start(bf16[16,128,128]{2,1,0:T(8,128)(2,1)S(1)} %get-tuple-element.34), channel_id=1, source_target_pairs={{0,1},{1,2},{2,3},{3,0},{4,5},{5,6},{6,7},{7,4},{8,9},{9,10},{10,1... | collective-permute-start | bytes 1572872 | tf_op jit(solution)/shard_map/ppermute | solution.py:181
  109.1 14.0 %collective-permute-start.20 = (bf16[16,128,128]{2,1,0:T(8,128)(2,1)S(1)}, bf16[16,128,128]{2,1,0:T(8,128)(2,1)S(1)}, u32[]{:S(2)}, u32[]{:S(2)}) collective-permute-start(bf16[16,128,128]{2,1,0:T(8,128)(2,1)S(1)} %get-tuple-element.35), channel_id=1, source_target_pairs={{0,3},{1,0},{2,1},{3,2},{4,7},{5,4},{6,5},{7,6},{8,11},{9,8},{10,9... | collective-permute-start | bytes 1572872 | tf_op jit(solution)/shard_map/ppermute | solution.py:181
  111.2 20.8 %collective-permute-start.21 = (bf16[16,128,128]{2,1,0:T(8,128)(2,1)S(1)}, bf16[16,128,128]{2,1,0:T(8,128)(2,1)S(1)}, u32[]{:S(2)}, u32[]{:S(2)}) collective-permute-start(bf16[16,128,128]{2,1,0:T(8,128)(2,1)S(1)} %get-tuple-element.36), channel_id=1, source_target_pairs={{0,2},{1,3},{2,0},{3,1},{4,6},{5,7},{6,4},{7,5},{8,10},{9,11},{10,... | collective-permute-start | bytes 1572872 | tf_op jit(solution)/shard_map/ppermute | solution.py:181
  134.3 59.6 %all-to-all-start = ((bf16[64,128,128]{2,1,0:T(8,128)(2,1)}), bf16[64,128,128]{2,1,0:T(8,128)(2,1)S(1)}, u32[]{:S(2)}, u32[]{:S(2)}) async-start(bf16[64,128,128]{2,1,0:T(8,128)(2,1)} %shard_map.50), calls=%async_computation | async-start | bytes 4194304 | tf_op jit(solution)/shard_map/all_to_all | solution.py:277
  (3 other events, 22.7 us)

commit v5 on v4

--- a/solution.py
+++ b/solution.py
@@ -125,7 +125,7 @@
     )(entry, keep, *blocks, cot)
 
 
-def arrange(index, sources, counts, into_source_order=False, outside=pl.ANY):
+def arrange(index, sources, counts, into_source_order=False, vmem_mb=16):
     given, total = sum(source.shape[0] for source in sources), sum(counts)
 
     def kernel(index_ref, *refs):
@@ -162,11 +162,11 @@
         kernel,
         out_shape=[jax.ShapeDtypeStruct((count, *shape), dtype) for count in counts],
         in_specs=[pl.BlockSpec(memory_space=pltpu.SMEM)]
-        + [pl.BlockSpec(memory_space=outside)] * len(sources),
-        out_specs=[pl.BlockSpec(memory_space=outside)] * len(counts),
+        + [pl.BlockSpec(memory_space=pl.ANY)] * len(sources),
+        out_specs=[pl.BlockSpec(memory_space=pl.ANY)] * len(counts),
         scratch_shapes=[pltpu.VMEM((given, *shape), dtype), pltpu.VMEM((total, *shape), dtype)]
         + [pltpu.SemaphoreType.DMA((len(sources),)), pltpu.SemaphoreType.DMA((len(counts),))],
-        compiler_params=pltpu.CompilerParams(vmem_limit_bytes=16 << 20),
+        compiler_params=pltpu.CompilerParams(vmem_limit_bytes=vmem_mb << 20),
         cost_estimate=pl.CostEstimate(flops=0, bytes_accessed=4 << 20, transcendentals=0),
     )(index, *sources)
 
@@ -246,17 +246,17 @@
     end = FIRST_LATE + LATE
     early_slots = jnp.concatenate([slots[:, :, :FIRST_LATE], slots[:, :, end:]], axis=2)
 
-    def over_x_and_core(sources, wanted):
+    def over_x_and_core(sources, wanted, vmem_mb):
         size = wanted.shape[2]
         wanted = wanted + slot_count * jnp.arange(size)
         order = jnp.concatenate([wanted[i].reshape(-1) for i in (1, 3, 2, 0)])
-        ahead, behind, across, own = arrange(order, sources, [nk * size] * nx)
+        ahead, behind, across, own = arrange(order, sources, [nk * size] * nx, vmem_mb=vmem_mb)
         came = [shift(ahead, "x", 1), shift(behind, "x", -1), shift(across, "x", 2), own]
         other = jnp.concatenate([part[size:] for part in came])
         return [*came, shift(other, "core", 1)]
 
-    held = over_x_and_core(early, early_slots)
-    held = held + over_x_and_core(late, slots[:, :, FIRST_LATE:end])
+    held = over_x_and_core(early, early_slots, 56)
+    held = held + over_x_and_core(late, slots[:, :, FIRST_LATE:end], 16)
 
     routes = [(step, room // 1) for step in (1, -1, 2) for _ in range(1)]
     counts = [count for _, count in routes] + [room]

time: 197 us -> 197 us (level)
  transfers between devices with their start and end apart: 23 -> 23, of which waited for: 10 -> 10; matrix products, arithmetic and copies ran while one was open for 3% -> 4% of each run, Pallas kernels for 2% -> 3%
where the time goes in v5:
time: 197 us
  waiting for transfers between devices  112 us (57%)
  starting transfers between devices  50.1 us (25%)
  Pallas kernels  24.6 us (12%)
  other arithmetic  4.43 us (2%)
  local copies, waits for them, and re-layouts  3.83 us (2%)
    ppermute x22, waiting for transfers between devices, shift(): lax.ppermute(blocks, axis, [(i, (i + step) % count) for i in range(count)])  61.6 us
    all_to_all x1, waiting for transfers between devices, shards(): lax.all_to_all(held, AXES[:3], split_axis=0, concat_axis=0, tiled=True)  50.9 us
    ppermute x22, starting transfers between devices, shift(): lax.ppermute(blocks, axis, [(i, (i + step) % count) for i in range(count)])  41.8 us
    pallas_call x1, Pallas kernels, adjoint_pieces(): pl.pallas_call(functools.partial(adjoint_kernel, span, arrays), out_shape...  13.5 us
    pallas_call x4, Pallas kernels, arrange(): pl.pallas_call(kernel, out_shape=[jax.ShapeDtypeStruct((count, *shape), d...  11.1 us
    all_to_all x1, starting transfers between devices, shards(): lax.all_to_all(held, AXES[:3], split_axis=0, concat_axis=0, tiled=True)  8.31 us
  transfers between devices with their start and end apart: 23, of which 10 were waited for; matrix products, arithmetic and copies ran while one was open for 4% of the time, Pallas kernels for 3%

profile of v5, /device:TPU:1, one launch (start us, length us, event | category | flops | bytes accessed | tf_op | source)
XLA Modules:
  0.0 197.2 jit_solution(217343266218444902)
XLA Ops:
  0.0 6.4 %collective-permute-start = (bf16[12,128,128]{2,1,0:T(8,128)(2,1)}, bf16[12,128,128]{2,1,0:T(8,128)(2,1)S(1)}, u32[]{:S(2)}, u32[]{:S(2)}) collective-permute-start(bf16[12,128,128]{2,1,0:T(8,128)(2,1)} %refs_0_.1), channel_id=1, source_target_pairs={{0,56},{8,0},{16,8},{24,16},{32,24},{40,32},{48,40},{56,48},{1,57}... | collective-permute-start | bytes 1179656 | tf_op jit(solution)/shard_map/ppermute | solution.py:181
  8.6 5.9 %collective-permute-done.refs_1_ = bf16[12,128,128]{2,1,0:T(8,128)(2,1)S(1)} collective-permute-done((bf16[12,128,128]{2,1,0:T(8,128)(2,1)}, bf16[12,128,128]{2,1,0:T(8,128)(2,1)S(1)}, u32[]{:S(2)}, u32[]{:S(2)}) %collective-permute-start) | collective-permute-done | bytes 393248 | tf_op jit(solution)/shard_map/ppermute | solution.py:181
  14.5 3.3 %collective-permute-start.1 = (bf16[12,128,128]{2,1,0:T(8,128)(2,1)S(1)}, bf16[12,128,128]{2,1,0:T(8,128)(2,1)S(1)}, u32[]{:S(2)}, u32[]{:S(2)}) collective-permute-start(bf16[12,128,128]{2,1,0:T(8,128)(2,1)S(1)} %collective-permute-done.refs_1_), channel_id=1, source_target_pairs={{0,56},{8,0},{16,8},{24,16},{32,24},{40,32},{48,40},{56,48},{1,57}... | collective-permute-start | bytes 1179656 | tf_op jit(solution)/shard_map/ppermute | solution.py:181
  19.1 5.5 %collective-permute-done.1.refs_2_ = bf16[12,128,128]{2,1,0:T(8,128)(2,1)S(1)} collective-permute-done((bf16[12,128,128]{2,1,0:T(8,128)(2,1)S(1)}, bf16[12,128,128]{2,1,0:T(8,128)(2,1)S(1)}, u32[]{:S(2)}, u32[]{:S(2)}) %collective-permute-start.1) | collective-permute-done | bytes 393248 | tf_op jit(solution)/shard_map/ppermute | solution.py:181
  24.7 3.4 %collective-permute-start.8 = (bf16[12,128,128]{2,1,0:T(8,128)(2,1)S(1)}, bf16[12,128,128]{2,1,0:T(8,128)(2,1)S(1)}, u32[]{:S(2)}, u32[]{:S(2)}) collective-permute-start(bf16[12,128,128]{2,1,0:T(8,128)(2,1)S(1)} %collective-permute-done.1.refs_2_), channel_id=1, source_target_pairs={{0,56},{8,0},{16,8},{24,16},{32,24},{40,32},{48,40},{56,48},{1,57}... | collective-permute-start | bytes 1179656 | tf_op jit(solution)/shard_map/ppermute | solution.py:181
  28.9 3.3 %shard_map.46 = (bf16[10,128,128]{2,1,0:T(8,128)(2,1)}, bf16[10,128,128]{2,1,0:T(8,128)(2,1)}, bf16[10,128,128]{2,1,0:T(8,128)(2,1)}, bf16[10,128,128]{2,1,0:T(8,128)(2,1)}) custom-call(s32[40]{0:T(128)} %pad_add_fusion.5.index_ref, bf16[12,128,128]{2,1,0:T(8,128)(2,1)} %refs_0_.1, bf16[12,128,128]{2,1,0:T(8,128)(2,1)} %copy-done.2, ...), custom_call_target="tpu_custom_call" | custom-call | bytes 4194304 | tf_op jit(solution)/shard_map/pallas_call | solution.py:161
  36.6 2.7 %collective-permute-start.11 = (bf16[6,128,128]{2,1,0:T(8,128)(2,1)S(1)}, bf16[6,128,128]{2,1,0:T(8,128)(2,1)S(1)}, u32[]{:S(2)}, u32[]{:S(2)}) collective-permute-start(bf16[6,128,128]{2,1,0:T(8,128)(2,1)S(1)} %slice.151), channel_id=1, source_target_pairs={{0,56},{8,0},{16,8},{24,16},{32,24},{40,32},{48,40},{56,48},{1,57}... | collective-permute-start | bytes 589832 | tf_op jit(solution)/shard_map/ppermute | solution.py:181
  39.4 2.5 %collective-permute-done.11.refs_2_ = bf16[6,128,128]{2,1,0:T(8,128)(2,1)S(1)} collective-permute-done((bf16[6,128,128]{2,1,0:T(8,128)(2,1)S(1)}, bf16[6,128,128]{2,1,0:T(8,128)(2,1)S(1)}, u32[]{:S(2)}, u32[]{:S(2)}) %collective-permute-start.11) | collective-permute-done | bytes 196640 | tf_op jit(solution)/shard_map/ppermute | solution.py:181
  41.9 3.5 %collective-permute-done.10.refs_1_ = bf16[6,128,128]{2,1,0:T(8,128)(2,1)S(1)} collective-permute-done((bf16[6,128,128]{2,1,0:T(8,128)(2,1)S(1)}, bf16[6,128,128]{2,1,0:T(8,128)(2,1)S(1)}, u32[]{:S(2)}, u32[]{:S(2)}) %collective-permute-start.10) | collective-permute-done | bytes 196640 | tf_op jit(solution)/shard_map/ppermute | solution.py:181
  45.4 2.6 %shard_map.47 = (bf16[6,128,128]{2,1,0:T(8,128)(2,1)S(1)}, bf16[6,128,128]{2,1,0:T(8,128)(2,1)S(1)}, bf16[6,128,128]{2,1,0:T(8,128)(2,1)S(1)}, bf16[6,128,128]{2,1,0:T(8,128)(2,1)S(1)}) custom-call(s32[24]{0:T(128)S(1)} %pad_add_fusion.6.index_ref, bf16[12,128,128]{2,1,0:T(8,128)(2,1)S(1)} %collective-permute-done.8.refs_0_, ...), custom_call_target="tpu_custom_call" | custom-call | bytes 4194304 | tf_op jit(solution)/shard_map/pallas_call | solution.py:161
  48.2 2.7 %collective-permute-start.13 = (bf16[6,128,128]{2,1,0:T(8,128)(2,1)S(1)}, bf16[6,128,128]{2,1,0:T(8,128)(2,1)S(1)}, u32[]{:S(2)}, u32[]{:S(2)}) collective-permute-start(bf16[6,128,128]{2,1,0:T(8,128)(2,1)S(1)} %get-tuple-element.27), channel_id=1, source_target_pairs={{0,192},{64,0},{128,64},{192,128},{1,193},{65,1},{129,65},{193,129... | collective-permute-start | bytes 589832 | tf_op jit(solution)/shard_map/ppermute | solution.py:181
  51.9 6.1 %collective-permute-start.7 = (bf16[20,128,128]{2,1,0:T(8,128)(2,1)}, bf16[20,128,128]{2,1,0:T(8,128)(2,1)S(1)}, u32[]{:S(2)}, u32[]{:S(2)}) collective-permute-start(bf16[20,128,128]{2,1,0:T(8,128)(2,1)} %pad_maximum_fusion), channel_id=1, source_target_pairs={{0,4},{4,0},{1,5},{5,1},{2,6},{6,2},{3,7},{7,3},{8,12},{12,8},{9,1... | collective-permute-start | bytes 1966088 | tf_op jit(solution)/shard_map/ppermute | solution.py:181
  58.9 5.5 %collective-permute-start.15 = (bf16[12,128,128]{2,1,0:T(8,128)(2,1)}, bf16[12,128,128]{2,1,0:T(8,128)(2,1)S(1)}, u32[]{:S(2)}, u32[]{:S(2)}) collective-permute-start(bf16[12,128,128]{2,1,0:T(8,128)(2,1)} %pad_maximum_fusion.1), channel_id=1, source_target_pairs={{0,4},{4,0},{1,5},{5,1},{2,6},{6,2},{3,7},{7,3},{8,12},{12,8},{9,1... | collective-permute-start | bytes 1179656 | tf_op jit(solution)/shard_map/ppermute | solution.py:181
  65.9 2.9 %shard_map.48 = (bf16[16,128,128]{2,1,0:T(8,128)(2,1)S(1)}, bf16[16,128,128]{2,1,0:T(8,128)(2,1)S(1)}, bf16[16,128,128]{2,1,0:T(8,128)(2,1)S(1)}, bf16[16,128,128]{2,1,0:T(8,128)(2,1)S(1)}) custom-call(s32[64]{0:T(128)S(1)} %pad_add_fusion.4.index_ref, bf16[10,128,128]{2,1,0:T(8,128)(2,1)S(1)} %collective-permute-done.4.refs_0_, ...), custom_call_target="tpu_custom_call" | custom-call | bytes 4194304 | tf_op jit(solution)/shard_map/pallas_call | solution.py:161
  71.7 1.6 collective-permute-start.18
  73.5 9.8 %collective-permute-done.16.refs_0_ = bf16[16,128,128]{2,1,0:T(8,128)(2,1)S(1)} collective-permute-done((bf16[16,128,128]{2,1,0:T(8,128)(2,1)S(1)}, bf16[16,128,128]{2,1,0:T(8,128)(2,1)S(1)}, u32[]{:S(2)}, u32[]{:S(2)}) %collective-permute-start.16) | collective-permute-done | bytes 524320 | tf_op jit(solution)/shard_map/ppermute | solution.py:181
  83.4 12.3 %collective-permute-done.18.refs_2_ = bf16[16,128,128]{2,1,0:T(8,128)(2,1)S(1)} collective-permute-done((bf16[16,128,128]{2,1,0:T(8,128)(2,1)S(1)}, bf16[16,128,128]{2,1,0:T(8,128)(2,1)S(1)}, u32[]{:S(2)}, u32[]{:S(2)}) %collective-permute-start.18) | collective-permute-done | bytes 524320 | tf_op jit(solution)/shard_map/ppermute | solution.py:181
  95.7 13.5 %shard_map.49 = (bf16[16,128,128]{2,1,0:T(8,128)(2,1)S(1)}, bf16[16,128,128]{2,1,0:T(8,128)(2,1)S(1)}, bf16[16,128,128]{2,1,0:T(8,128)(2,1)S(1)}, bf16[16,128,128]{2,1,0:T(8,128)(2,1)S(1)}) custom-call(s32[2,64]{1,0:T(2,128)S(1)} %pad_add_fusion.2.entry_ref, s32[64]{0:T(128)S(1)} %reshape.299.keep_ref, ...), custom_call_target="tpu_custom_call" | custom-call | flops 11000000512 | bytes 5242880 | tf_op jit(solution)/shard_map/pallas_call | solution.py:114
  109.8 2.2 %collective-permute-start.20 = (bf16[16,128,128]{2,1,0:T(8,128)(2,1)S(1)}, bf16[16,128,128]{2,1,0:T(8,128)(2,1)S(1)}, u32[]{:S(2)}, u32[]{:S(2)}) collective-permute-start(bf16[16,128,128]{2,1,0:T(8,128)(2,1)S(1)} %get-tuple-element.35), channel_id=1, source_target_pairs={{0,3},{1,0},{2,1},{3,2},{4,7},{5,4},{6,5},{7,6},{8,11},{9,8},{10,9... | collective-permute-start | bytes 1572872 | tf_op jit(solution)/shard_map/ppermute | solution.py:181
  112.2 11.9 %collective-permute-done.19.refs_0_ = bf16[16,128,128]{2,1,0:T(8,128)(2,1)S(1)} collective-permute-done((bf16[16,128,128]{2,1,0:T(8,128)(2,1)S(1)}, bf16[16,128,128]{2,1,0:T(8,128)(2,1)S(1)}, u32[]{:S(2)}, u32[]{:S(2)}) %collective-permute-start.19) | collective-permute-done | bytes 524320 | tf_op jit(solution)/shard_map/ppermute | solution.py:181
  124.0 8.8 %collective-permute-done.21.refs_2_ = bf16[16,128,128]{2,1,0:T(8,128)(2,1)S(1)} collective-permute-done((bf16[16,128,128]{2,1,0:T(8,128)(2,1)S(1)}, bf16[16,128,128]{2,1,0:T(8,128)(2,1)S(1)}, u32[]{:S(2)}, u32[]{:S(2)}) %collective-permute-start.21) | collective-permute-done | bytes 524320 | tf_op jit(solution)/shard_map/ppermute | solution.py:181
  132.9 2.2 %shard_map.50 = bf16[64,128,128]{2,1,0:T(8,128)(2,1)} custom-call(s32[64]{0:T(128)S(1)} %pad_add_fusion.3.index_ref, bf16[16,128,128]{2,1,0:T(8,128)(2,1)S(1)} %collective-permute-done.19.refs_0_, bf16[16,128,128]{2,1,0:T(8,128)(2,1)S(1)} %collective-permute-done.20.refs_1_, bf16[16,128,128]{2,1,0:T(8,128)(2,1)S(1)} %collective-permute-done.21.refs_2_, ...), custom_call_target="tpu_custom_call" | custom-call | bytes 4194304 | tf_op jit(solution)/shard_map/pallas_call | solution.py:161
  135.1 8.3 %all-to-all-start = ((bf16[64,128,128]{2,1,0:T(8,128)(2,1)}), bf16[64,128,128]{2,1,0:T(8,128)(2,1)S(1)}, u32[]{:S(2)}, u32[]{:S(2)}) async-start(bf16[64,128,128]{2,1,0:T(8,128)(2,1)} %shard_map.50), calls=%async_computation | async-start | bytes 4194304 | tf_op jit(solution)/shard_map/all_to_all | solution.py:277
  143.8 50.9 %all-to-all-done = bf16[64,128,128]{2,1,0:T(8,128)(2,1)S(1)} async-done(((bf16[64,128,128]{2,1,0:T(8,128)(2,1)}), bf16[64,128,128]{2,1,0:T(8,128)(2,1)S(1)}, u32[]{:S(2)}, u32[]{:S(2)}) %all-to-all-start) | async-done | bytes 2097184 | tf_op jit(solution)/shard_map/all_to_all | solution.py:277
  (118 shorter events, 18.6 us)
Async XLA Ops:
  0.0 14.5 %collective-permute-start = (bf16[12,128,128]{2,1,0:T(8,128)(2,1)}, bf16[12,128,128]{2,1,0:T(8,128)(2,1)S(1)}, u32[]{:S(2)}, u32[]{:S(2)}) collective-permute-start(bf16[12,128,128]{2,1,0:T(8,128)(2,1)} %refs_0_.1), channel_id=1, source_target_pairs={{0,56},{8,0},{16,8},{24,16},{32,24},{40,32},{48,40},{56,48},{1,57}... | collective-permute-start | bytes 1179656 | tf_op jit(solution)/shard_map/ppermute | solution.py:181
  6.4 11.4 %collective-permute-start.2 = (bf16[12,128,128]{2,1,0:T(8,128)(2,1)}, bf16[12,128,128]{2,1,0:T(8,128)(2,1)S(1)}, u32[]{:S(2)}, u32[]{:S(2)}) collective-permute-start(bf16[12,128,128]{2,1,0:T(8,128)(2,1)} %refs_0_.1), channel_id=1, source_target_pairs={{0,8},{8,16},{16,24},{24,32},{32,40},{40,48},{48,56},{56,0},{1,9},... | collective-permute-start | bytes 1179656 | tf_op jit(solution)/shard_map/ppermute | solution.py:181
  14.5 10.2 %collective-permute-start.1 = (bf16[12,128,128]{2,1,0:T(8,128)(2,1)S(1)}, bf16[12,128,128]{2,1,0:T(8,128)(2,1)S(1)}, u32[]{:S(2)}, u32[]{:S(2)}) collective-permute-start(bf16[12,128,128]{2,1,0:T(8,128)(2,1)S(1)} %collective-permute-done.refs_1_), channel_id=1, source_target_pairs={{0,56},{8,0},{16,8},{24,16},{32,24},{40,32},{48,40},{56,48},{1,57}... | collective-permute-start | bytes 1179656 | tf_op jit(solution)/shard_map/ppermute | solution.py:181
  17.8 10.3 %collective-permute-start.3 = (bf16[12,128,128]{2,1,0:T(8,128)(2,1)S(1)}, bf16[12,128,128]{2,1,0:T(8,128)(2,1)S(1)}, u32[]{:S(2)}, u32[]{:S(2)}) collective-permute-start(bf16[12,128,128]{2,1,0:T(8,128)(2,1)S(1)} %collective-permute-done.2.refs_4_), channel_id=1, source_target_pairs={{0,8},{8,16},{16,24},{24,32},{32,40},{40,48},{48,56},{56,0},{1,9},... | collective-permute-start | bytes 1179656 | tf_op jit(solution)/shard_map/ppermute | solution.py:181
  24.7 11.9 %collective-permute-start.8 = (bf16[12,128,128]{2,1,0:T(8,128)(2,1)S(1)}, bf16[12,128,128]{2,1,0:T(8,128)(2,1)S(1)}, u32[]{:S(2)}, u32[]{:S(2)}) collective-permute-start(bf16[12,128,128]{2,1,0:T(8,128)(2,1)S(1)} %collective-permute-done.1.refs_2_), channel_id=1, source_target_pairs={{0,56},{8,0},{16,8},{24,16},{32,24},{40,32},{48,40},{56,48},{1,57}... | collective-permute-start | bytes 1179656 | tf_op jit(solution)/shard_map/ppermute | solution.py:181
  28.1 11.2 %collective-permute-start.9 = (bf16[12,128,128]{2,1,0:T(8,128)(2,1)S(1)}, bf16[12,128,128]{2,1,0:T(8,128)(2,1)S(1)}, u32[]{:S(2)}, u32[]{:S(2)}) collective-permute-start(bf16[12,128,128]{2,1,0:T(8,128)(2,1)S(1)} %collective-permute-done.3.refs_3_), channel_id=1, source_target_pairs={{0,8},{8,16},{16,24},{24,32},{32,40},{40,48},{48,56},{56,0},{1,9},... | collective-permute-start | bytes 1179656 | tf_op jit(solution)/shard_map/ppermute | solution.py:181
  32.2 18.6 %collective-permute-start.4 = (bf16[10,128,128]{2,1,0:T(8,128)(2,1)}, bf16[10,128,128]{2,1,0:T(8,128)(2,1)S(1)}, u32[]{:S(2)}, u32[]{:S(2)}) collective-permute-start(bf16[10,128,128]{2,1,0:T(8,128)(2,1)} %get-tuple-element.22), channel_id=1, source_target_pairs={{0,64},{64,128},{128,192},{192,0},{1,65},{65,129},{129,193},{193,1... | collective-permute-start | bytes 983048 | tf_op jit(solution)/shard_map/ppermute | solution.py:181
  33.6 17.3 %collective-permute-start.5 = (bf16[10,128,128]{2,1,0:T(8,128)(2,1)}, bf16[10,128,128]{2,1,0:T(8,128)(2,1)S(1)}, u32[]{:S(2)}, u32[]{:S(2)}) collective-permute-start(bf16[10,128,128]{2,1,0:T(8,128)(2,1)} %get-tuple-element.23), channel_id=1, source_target_pairs={{0,192},{64,0},{128,64},{192,128},{1,193},{65,1},{129,65},{193,129... | collective-permute-start | bytes 983048 | tf_op jit(solution)/shard_map/ppermute | solution.py:181
  35.1 15.9 %collective-permute-start.6 = (bf16[10,128,128]{2,1,0:T(8,128)(2,1)}, bf16[10,128,128]{2,1,0:T(8,128)(2,1)S(1)}, u32[]{:S(2)}, u32[]{:S(2)}) collective-permute-start(bf16[10,128,128]{2,1,0:T(8,128)(2,1)} %get-tuple-element.24), channel_id=1, source_target_pairs={{0,128},{64,192},{128,0},{192,64},{1,129},{65,193},{129,1},{193,65... | collective-permute-start | bytes 983048 | tf_op jit(solution)/shard_map/ppermute | solution.py:181
  36.6 5.3 %collective-permute-start.11 = (bf16[6,128,128]{2,1,0:T(8,128)(2,1)S(1)}, bf16[6,128,128]{2,1,0:T(8,128)(2,1)S(1)}, u32[]{:S(2)}, u32[]{:S(2)}) collective-permute-start(bf16[6,128,128]{2,1,0:T(8,128)(2,1)S(1)} %slice.151), channel_id=1, source_target_pairs={{0,56},{8,0},{16,8},{24,16},{32,24},{40,32},{48,40},{56,48},{1,57}... | collective-permute-start | bytes 589832 | tf_op jit(solution)/shard_map/ppermute | solution.py:181
  39.3 6.1 %collective-permute-start.10 = (bf16[6,128,128]{2,1,0:T(8,128)(2,1)S(1)}, bf16[6,128,128]{2,1,0:T(8,128)(2,1)S(1)}, u32[]{:S(2)}, u32[]{:S(2)}) collective-permute-start(bf16[6,128,128]{2,1,0:T(8,128)(2,1)S(1)} %slice.150), channel_id=1, source_target_pairs={{0,8},{8,16},{16,24},{24,32},{32,40},{40,48},{48,56},{56,0},{1,9},... | collective-permute-start | bytes 589832 | tf_op jit(solution)/shard_map/ppermute | solution.py:181
  48.1 9.9 %collective-permute-start.12 = (bf16[6,128,128]{2,1,0:T(8,128)(2,1)S(1)}, bf16[6,128,128]{2,1,0:T(8,128)(2,1)S(1)}, u32[]{:S(2)}, u32[]{:S(2)}) collective-permute-start(bf16[6,128,128]{2,1,0:T(8,128)(2,1)S(1)} %get-tuple-element.26), channel_id=1, source_target_pairs={{0,64},{64,128},{128,192},{192,0},{1,65},{65,129},{129,193},{193,1... | collective-permute-start | bytes 589832 | tf_op jit(solution)/shard_map/ppermute | solution.py:181
  48.2 9.8 %collective-permute-start.13 = (bf16[6,128,128]{2,1,0:T(8,128)(2,1)S(1)}, bf16[6,128,128]{2,1,0:T(8,128)(2,1)S(1)}, u32[]{:S(2)}, u32[]{:S(2)}) collective-permute-start(bf16[6,128,128]{2,1,0:T(8,128)(2,1)S(1)} %get-tuple-element.27), channel_id=1, source_target_pairs={{0,192},{64,0},{128,64},{192,128},{1,193},{65,1},{129,65},{193,129... | collective-permute-start | bytes 589832 | tf_op jit(solution)/shard_map/ppermute | solution.py:181
  50.8 7.2 %collective-permute-start.14 = (bf16[6,128,128]{2,1,0:T(8,128)(2,1)S(1)}, bf16[6,128,128]{2,1,0:T(8,128)(2,1)S(1)}, u32[]{:S(2)}, u32[]{:S(2)}) collective-permute-start(bf16[6,128,128]{2,1,0:T(8,128)(2,1)S(1)} %get-tuple-element.28), channel_id=1, source_target_pairs={{0,128},{64,192},{128,0},{192,64},{1,129},{65,193},{129,1},{193,65... | collective-permute-start | bytes 589832 | tf_op jit(solution)/shard_map/ppermute | solution.py:181
  51.9 12.9 %collective-permute-start.7 = (bf16[20,128,128]{2,1,0:T(8,128)(2,1)}, bf16[20,128,128]{2,1,0:T(8,128)(2,1)S(1)}, u32[]{:S(2)}, u32[]{:S(2)}) collective-permute-start(bf16[20,128,128]{2,1,0:T(8,128)(2,1)} %pad_maximum_fusion), channel_id=1, source_target_pairs={{0,4},{4,0},{1,5},{5,1},{2,6},{6,2},{3,7},{7,3},{8,12},{12,8},{9,1... | collective-permute-start | bytes 1966088 | tf_op jit(solution)/shard_map/ppermute | solution.py:181
  58.0 37.7 %copy-start.1 = (bf16[1024,128]{1,0:T(8,128)(2,1)S(1)}, bf16[1024,128]{1,0:T(8,128)(2,1)}, u32[]{:S(2)}) copy-start(bf16[1024,128]{1,0:T(8,128)(2,1)} %refs_4_.1) | copy-start | bytes 786436
  58.9 7.1 %collective-permute-start.15 = (bf16[12,128,128]{2,1,0:T(8,128)(2,1)}, bf16[12,128,128]{2,1,0:T(8,128)(2,1)S(1)}, u32[]{:S(2)}, u32[]{:S(2)}) collective-permute-start(bf16[12,128,128]{2,1,0:T(8,128)(2,1)} %pad_maximum_fusion.1), channel_id=1, source_target_pairs={{0,4},{4,0},{1,5},{5,1},{2,6},{6,2},{3,7},{7,3},{8,12},{12,8},{9,1... | collective-permute-start | bytes 1179656 | tf_op jit(solution)/shard_map/ppermute | solution.py:181
  68.8 14.6 %collective-permute-start.16 = (bf16[16,128,128]{2,1,0:T(8,128)(2,1)S(1)}, bf16[16,128,128]{2,1,0:T(8,128)(2,1)S(1)}, u32[]{:S(2)}, u32[]{:S(2)}) collective-permute-start(bf16[16,128,128]{2,1,0:T(8,128)(2,1)S(1)} %get-tuple-element.30), channel_id=1, source_target_pairs={{0,1},{1,2},{2,3},{3,0},{4,5},{5,6},{6,7},{7,4},{8,9},{9,10},{10,1... | collective-permute-start | bytes 1572872 | tf_op jit(solution)/shard_map/ppermute | solution.py:181
  70.2 13.2 %collective-permute-start.17 = (bf16[16,128,128]{2,1,0:T(8,128)(2,1)S(1)}, bf16[16,128,128]{2,1,0:T(8,128)(2,1)S(1)}, u32[]{:S(2)}, u32[]{:S(2)}) collective-permute-start(bf16[16,128,128]{2,1,0:T(8,128)(2,1)S(1)} %get-tuple-element.31), channel_id=1, source_target_pairs={{0,3},{1,0},{2,1},{3,2},{4,7},{5,4},{6,5},{7,6},{8,11},{9,8},{10,9... | collective-permute-start | bytes 1572872 | tf_op jit(solution)/shard_map/ppermute | solution.py:181
  71.7 24.0 %collective-permute-start.18 = (bf16[16,128,128]{2,1,0:T(8,128)(2,1)S(1)}, bf16[16,128,128]{2,1,0:T(8,128)(2,1)S(1)}, u32[]{:S(2)}, u32[]{:S(2)}) collective-permute-start(bf16[16,128,128]{2,1,0:T(8,128)(2,1)S(1)} %get-tuple-element.32), channel_id=1, source_target_pairs={{0,2},{1,3},{2,0},{3,1},{4,6},{5,7},{6,4},{7,5},{8,10},{9,11},{10,... | collective-permute-start | bytes 1572872 | tf_op jit(solution)/shard_map/ppermute | solution.py:181
  109.3 14.8 %collective-permute-start.19 = (bf16[16,128,128]{2,1,0:T(8,128)(2,1)S(1)}, bf16[16,128,128]{2,1,0:T(8,128)(2,1)S(1)}, u32[]{:S(2)}, u32[]{:S(2)}) collective-permute-start(bf16[16,128,128]{2,1,0:T(8,128)(2,1)S(1)} %get-tuple-element.34), channel_id=1, source_target_pairs={{0,1},{1,2},{2,3},{3,0},{4,5},{5,6},{6,7},{7,4},{8,9},{9,10},{10,1... | collective-permute-start | bytes 1572872 | tf_op jit(solution)/shard_map/ppermute | solution.py:181
  109.8 14.2 %collective-permute-start.20 = (bf16[16,128,128]{2,1,0:T(8,128)(2,1)S(1)}, bf16[16,128,128]{2,1,0:T(8,128)(2,1)S(1)}, u32[]{:S(2)}, u32[]{:S(2)}) collective-permute-start(bf16[16,128,128]{2,1,0:T(8,128)(2,1)S(1)} %get-tuple-element.35), channel_id=1, source_target_pairs={{0,3},{1,0},{2,1},{3,2},{4,7},{5,4},{6,5},{7,6},{8,11},{9,8},{10,9... | collective-permute-start | bytes 1572872 | tf_op jit(solution)/shard_map/ppermute | solution.py:181
  112.0 20.9 %collective-permute-start.21 = (bf16[16,128,128]{2,1,0:T(8,128)(2,1)S(1)}, bf16[16,128,128]{2,1,0:T(8,128)(2,1)S(1)}, u32[]{:S(2)}, u32[]{:S(2)}) collective-permute-start(bf16[16,128,128]{2,1,0:T(8,128)(2,1)S(1)} %get-tuple-element.36), channel_id=1, source_target_pairs={{0,2},{1,3},{2,0},{3,1},{4,6},{5,7},{6,4},{7,5},{8,10},{9,11},{10,... | collective-permute-start | bytes 1572872 | tf_op jit(solution)/shard_map/ppermute | solution.py:181
  135.1 59.6 %all-to-all-start = ((bf16[64,128,128]{2,1,0:T(8,128)(2,1)}), bf16[64,128,128]{2,1,0:T(8,128)(2,1)S(1)}, u32[]{:S(2)}, u32[]{:S(2)}) async-start(bf16[64,128,128]{2,1,0:T(8,128)(2,1)} %shard_map.50), calls=%async_computation | async-start | bytes 4194304 | tf_op jit(solution)/shard_map/all_to_all | solution.py:277
  (7 other events, 70.8 us)
